TPU v7x, 32 devices: a whole 2x2x4 slice. The times are simulated.
32 devices in a mesh: blk: 4 (over y, core), grp: 2 (over x), tp: 4 (over z).
Axes of the slice: x: 2, y: 2, z: 4, core: 2. Of those that a mesh axis runs over, the one named last changes fastest.
Arguments:
- dispatched: bfloat16 [2048, 5120], P(('blk', 'grp'), 'tp'), may hold values from -6 to 6
- route_prob: bfloat16 [2048], P(('blk', 'grp')), may hold values from 0.099609375 to 1
- peer_rows: int32 [16], P(('blk', 'grp')), may hold values from 1 to 128, as said below
- gate_weight: bfloat16 [2, 5120, 768], P('grp', 'blk', 'tp'), may hold values from -0.078125 to 0.078125
- up_weight: bfloat16 [2, 5120, 768], P('grp', 'blk', 'tp'), may hold values from -0.078125 to 0.078125
- down_weight: bfloat16 [2, 768, 5120], P('grp', None, 'tp'), may hold values from -0.21875 to 0.21875
Outputs:
- expert_out: bfloat16 [2048, 5120], P(('blk', 'grp'), 'tp')
Inputs may be any that keep to these rules, and one draw needn't show every extreme that they name: `peer_rows`: in every draw one expert group receives 128 live rows from every source device.
All inputs are finite; a program needn't handle non-finite values.
Results may differ from a plain program's by a relative error of at most 0.0049.
Values may be sent and summed in bfloat16 or wider, within the bound.
No kernel may reach another device: no remote copies, remote signals or barrier semaphores. Data moves between devices by JAX's collectives and lax.ppermute only.
A program may use at most 64 MiB of HBM per device.

v0:
```python
import functools

import jax
import jax.numpy as jnp
from jax import lax
from jax.experimental import pallas as pl
from jax.experimental.pallas import tpu as pltpu
from jax.sharding import PartitionSpec as P

PARAMS = pltpu.CompilerParams(vmem_limit_bytes=6 << 20)
VMEM = pl.BlockSpec(memory_space=pltpu.VMEM)
WHOLE = pl.BlockSpec(memory_space=pl.ANY)
DMA = pltpu.SemaphoreType.DMA
AHEAD = 3
EXTRA = 16
DISTANCES = (0, 1, 3, 2)


def cost(flops, values, exps=0):
    return pl.CostEstimate(flops=flops, bytes_accessed=2 * values, transcendentals=exps)


def rows_at(index, size):
    return pl.ds(pl.multiple_of(index * size, size), size)


def after(x, *done):
    return lax.optimization_barrier((x, *done))[0]


def copy_all(pairs, sems):
    copies = [pltpu.make_async_copy(source, to, sems.at[i]) for i, (source, to) in enumerate(pairs)]
    for copy in copies:
        copy.start()
    for copy in copies:
        copy.wait()


def mine_kernel(tokens, out, sem):
    copy = pltpu.make_async_copy(tokens.at[rows_at(lax.axis_index("grp"), out.shape[0]), :], out, sem)
    copy.start()
    copy.wait()


def rest_kernel(groups, tokens, gate, up, first, *refs):
    outs, panel, sems = refs[: groups - 1], refs[groups - 1], refs[groups]
    group = lax.axis_index("grp")
    rows, hid = tokens.shape[0] // groups, gate.shape[0]
    pairs = [(tokens.at[rows_at(lax.rem(group + step, groups), rows), :], out) for step, out in enumerate(outs, 1)]
    copy_all(pairs + [(gate, panel.at[:hid, :]), (up, panel.at[hid:, :])], sems)


def prepare(tokens, gate, up, groups):
    rows, depth = tokens.shape
    hid, high = gate.shape
    block = jax.ShapeDtypeStruct((rows // groups, depth), tokens.dtype)
    tokens, gate, up = (pltpu.with_memory_space_constraint(x, pltpu.HBM) for x in (tokens, gate, up))
    mine = pl.pallas_call(
        mine_kernel,
        out_shape=block,
        in_specs=[WHOLE],
        out_specs=VMEM,
        scratch_shapes=[DMA],
        compiler_params=PARAMS,
        cost_estimate=cost(0, 2 * block.size),
        name="own_rows",
    )(tokens)
    *others, panel = pl.pallas_call(
        functools.partial(rest_kernel, groups),
        out_shape=[block] * (groups - 1) + [jax.ShapeDtypeStruct((2 * hid, high), gate.dtype)],
        in_specs=[WHOLE] * 4,
        out_specs=[VMEM] * groups,
        scratch_shapes=[DMA((groups + 1,))],
        compiler_params=PARAMS,
        cost_estimate=cost(0, 2 * rows * depth + 4 * high * hid),
        name="other_rows_and_weights",
    )(tokens, gate, up, mine)
    return [mine, *others], panel


def weigh_kernel(chances, counts, out):
    group, (groups, rows) = lax.axis_index("grp"), chances.shape
    every = chances[...].astype(jnp.float32)
    line = lax.broadcasted_iota(jnp.int32, every.shape, 0)
    slot = lax.broadcasted_iota(jnp.int32, (1, rows), 1)
    for step in range(groups):
        index = lax.rem(group + step, groups)
        chance = jnp.sum(jnp.where(line == index, every, 0.0), axis=0, keepdims=True)
        out[step : step + 1, :] = jnp.where(slot < counts[index], chance, 0.0)


def weigh(chances, counts):
    return pl.pallas_call(
        weigh_kernel,
        out_shape=jax.ShapeDtypeStruct(chances.shape, jnp.float32),
        in_specs=[VMEM, pl.BlockSpec(memory_space=pltpu.SMEM)],
        out_specs=VMEM,
        compiler_params=PARAMS,
        cost_estimate=cost(0, chances.size),
        name="weigh",
    )(chances, counts)


def attach_kernel(step, tokens, scales, out, sem):
    groups, rows = scales.shape
    index = lax.rem(lax.axis_index("grp") + step, groups)
    copy = pltpu.make_async_copy(tokens.at[rows_at(index, rows), :], out.at[:rows, :], sem)
    copy.start()
    lanes = out.shape[1]
    line = jnp.concatenate([scales[step : step + 1, :], jnp.zeros((1, lanes - rows), jnp.float32)], axis=1)
    out[rows:, :] = jnp.broadcast_to(line, (EXTRA, lanes)).astype(out.dtype)
    copy.wait()


def attach(step, tokens, scales):
    groups, rows = scales.shape
    depth = tokens.shape[1]
    return pl.pallas_call(
        functools.partial(attach_kernel, step),
        out_shape=jax.ShapeDtypeStruct((rows + EXTRA, depth), tokens.dtype),
        in_specs=[WHOLE, VMEM],
        out_specs=VMEM,
        scratch_shapes=[DMA],
        compiler_params=PARAMS,
        cost_estimate=cost(0, 2 * rows * depth),
        name="attach_weights",
    )(pltpu.with_memory_space_constraint(tokens, pltpu.HBM), scales)


def order_kernel(*refs):
    blocks, panel, sems = refs[:-2], refs[-2], refs[-1]
    mine = lax.axis_index("blk")
    copy_all([(block, panel.at[jnp.bitwise_xor(mine, j)]) for j, block in enumerate(blocks)], sems)


def in_order(blocks):
    n = len(blocks)
    return pl.pallas_call(
        order_kernel,
        out_shape=jax.ShapeDtypeStruct((n, *blocks[0].shape), blocks[0].dtype),
        in_specs=[WHOLE] * n,
        out_specs=VMEM,
        scratch_shapes=[DMA((n,))],
        compiler_params=PARAMS,
        cost_estimate=cost(0, 2 * n * blocks[0].size),
        name="weights_in_order",
    )(*blocks)


def swap(x, axis, bit):
    return lax.ppermute(x, axis, [(i, i ^ bit) for i in range(lax.axis_size(axis))])


def along(step, moves, straight=()):
    groups = lax.axis_size("grp")
    pairs = []
    for g in range(groups):
        pairs += [(g * 4 + a, (g + step) % groups * 4 + b) for a, b in moves]
        pairs += [(g * 4 + a, g * 4 + b) for a, b in straight]
    return pairs


def ring(block, step):
    right = lax.ppermute(block, ("grp", "tp"), along(step, [(i, (i + 1) % 4) for i in range(4)]))
    left = lax.ppermute(block, ("grp", "tp"), along(step, [(i, (i + 3) % 4) for i in range(4)]))
    return right, left


def choose_kernel(here, right, left, out):
    place = lax.axis_index("tp")
    inner = jnp.where(place == 2, right[...], left[...])
    out[...] = jnp.where(jnp.logical_or(place == 0, place == 3), here[...], inner)


def choose(here, right, left):
    return pl.pallas_call(
        choose_kernel,
        out_shape=jax.ShapeDtypeStruct(here.shape, here.dtype),
        in_specs=[VMEM] * 3,
        out_specs=VMEM,
        compiler_params=PARAMS,
        cost_estimate=cost(8000000000, 4 * here.size),
        name="choose",
    )(here, right, left)


def middle(block, step):
    return lax.ppermute(block, ("grp", "tp"), along(step, [(0, 2), (3, 1)], [(2, 3), (1, 0)]))


def product(panel, chunk, k):
    depth, high = chunk.shape[1], panel.shape[2]
    total = 0
    for i in range(depth // high):
        part = chunk[:, i * high : (i + 1) * high]
        total += lax.dot_general(
            panel[k * (depth // high) + i], part, (((1,), (1,)), ((), ())), preferred_element_type=jnp.float32
        )
    return total


def near_sum(place, panel, right, left):
    return product(panel, right[...], lax.rem(place + 3, 4)) + product(panel, left[...], lax.rem(place + 1, 4))


def finish(place, panel, total, x, opposite, weight):
    total += product(panel, x, place)
    total += product(panel, opposite, lax.rem(place + 2, 4))
    hid = total.shape[0] // 2
    gate, up = total[:hid], total[hid:]
    return gate / (1.0 + jnp.exp(-gate)) * up * weight


def hidden_kernel(panel, right, left, x, opposite, scales, *refs):
    place, count = lax.axis_index("tp"), len(refs) // 3
    others, out, sums = refs[: 2 * count], refs[2 * count], refs[2 * count + 1 :]
    total = near_sum(place, panel, right, left)
    out[...] = finish(place, panel, total, x[...], opposite[...], scales[:1, :]).astype(out.dtype)
    for i, to in enumerate(sums):
        to[...] = near_sum(place, panel, *others[2 * i : 2 * i + 2])


def finish_kernel(panel, total, x, opposite, out):
    rows = out.shape[1]
    weight = x[rows : rows + 1, :rows].astype(jnp.float32)
    out[...] = finish(lax.axis_index("tp"), panel, total[...], x[:rows, :], opposite[...], weight).astype(out.dtype)


def call_rows(kernel, chunks, name, outs, panel, *operands):
    share = chunks * panel.size // 4
    return pl.pallas_call(
        kernel,
        out_shape=outs,
        in_specs=[VMEM] * (1 + len(operands)),
        out_specs=[VMEM] * len(outs),
        compiler_params=PARAMS,
        cost_estimate=cost(2 * outs[0].shape[1] * share, share),
        name=name,
    )(panel, *operands)


def down_sum(hiddens, distances, down):
    place = lax.axis_index("tp")
    hid = hiddens[0].shape[0]
    total = 0
    for hidden, s in zip(hiddens, distances):
        part = down[rows_at(lax.rem(place - s + 4, 4), hid), :]
        total += lax.dot_general(hidden[...], part, (((0,), (0,)), ((), ())), preferred_element_type=jnp.float32)
    return total


def early_kernel(distances, *refs):
    refs[-1][...] = down_sum(refs[:-2], distances, refs[-2])


def down_kernel(step, groups, distances, *refs):
    count = len(distances)
    hiddens, down = refs[:count], refs[count]
    out, rows_here, sem = refs[-3:]
    group = lax.axis_index("grp")
    rows = hiddens[0].shape[1]
    total = down_sum(hiddens, distances, down)
    if count < 4:
        total += refs[count + 1][...]
    rows_here[...] = total.astype(rows_here.dtype)
    to = out.at[rows_at(lax.rem(group - step + groups, groups), rows), :]
    copy = pltpu.make_async_copy(rows_here, to, sem)
    copy.start()
    copy.wait()


def early_sum(hiddens, distances, down):
    rows, wide = hiddens[0].shape[1], down.shape[1]
    return pl.pallas_call(
        functools.partial(early_kernel, distances),
        out_shape=jax.ShapeDtypeStruct((rows, wide), jnp.float32),
        in_specs=[VMEM] * (len(hiddens) + 1),
        out_specs=VMEM,
        compiler_params=PARAMS,
        cost_estimate=cost(0, 0),
        name="early_down",
    )(*hiddens, down)


def project_down(step, groups, hiddens, down, out, ahead):
    rows, wide = hiddens[0].shape[1], down.shape[1]
    distances = DISTANCES
    earlier = [] if out is None else [out]
    sums = []
    if ahead:
        sums = [early_sum(hiddens[:ahead], distances[:ahead], down)]
        hiddens, distances = hiddens[ahead:], distances[ahead:]
    count = len(hiddens)
    return pl.pallas_call(
        functools.partial(down_kernel, step, groups, distances),
        out_shape=jax.ShapeDtypeStruct((groups * rows, wide), jnp.bfloat16),
        in_specs=[VMEM] * (count + 1 + len(sums)) + [WHOLE] * len(earlier),
        out_specs=WHOLE,
        scratch_shapes=[pltpu.VMEM((rows, wide), jnp.bfloat16), DMA],
        input_output_aliases={count + 1 + len(sums): 0} if earlier else {},
        compiler_params=PARAMS,
        cost_estimate=cost(rows * down.size if ahead else 8000000000, down.size + rows * wide),
        name="project_down",
    )(*hiddens, down, *sums, *earlier)


def everywhere(hidden):
    return [lax.ppermute(hidden, "tp", [(i, (i + s) % 4) for i in range(4)]) if s else hidden for s in DISTANCES]


def local(dispatched, route_prob, peer_rows, gate_weight, up_weight, down_weight):
    groups, blks = lax.axis_size("grp"), lax.axis_size("blk")
    per_peer = dispatched.shape[0] // groups
    hid = gate_weight.shape[2]

    rows, weight = prepare(dispatched, gate_weight[0].T, up_weight[0].T, groups)
    hops = [ring(rows[step], step) for step in range(groups)]
    opposites = [middle(choose(rows[step], *hops[step]), step) for step in range(groups)]

    scales = weigh(route_prob.reshape(groups, per_peer), peer_rows)
    for step in range(1, groups):
        block = attach(step, after(dispatched, *hops[0]), scales)
        rows[step] = lax.ppermute(block, "grp", [(i, (i + step) % groups) for i in range(groups)])

    have = {0: weight}
    bit = blks // 2
    while bit:
        for j in list(have):
            have[j ^ bit] = swap(have[j], "blk", bit)
        if bit == blks // 2:
            have[bit] = after(have[bit], *hops[0])
            have[0] = after(have[0], have[bit])
        bit //= 2
    panel = in_order([have[j] for j in range(blks)])

    sums = jax.ShapeDtypeStruct((2 * hid, per_peer), jnp.float32)
    hidden = jax.ShapeDtypeStruct((hid, per_peer), jnp.bfloat16)
    near = [chunk for hop in hops[1:] for chunk in hop]
    mine, *totals = call_rows(
        hidden_kernel, 4, "hidden_rows", [hidden] + [sums] * (groups - 1),
        panel, *hops[0], rows[0], opposites[0], scales, *near,
    )
    out = None
    for step in range(groups):
        done = mine
        if step:
            operands = totals[step - 1], rows[step], opposites[step]
            [done] = call_rows(finish_kernel, 2, "last_chunks", [hidden], panel, *operands)
        out = project_down(step, groups, everywhere(done), down_weight[0], out, AHEAD if step == groups - 1 else 0)
    return out


def solution(mesh):
    return jax.shard_map(
        local,
        mesh=mesh,
        in_specs=(
            P(("blk", "grp"), "tp"),
            P(("blk", "grp")),
            P(("blk", "grp")),
            P("grp", "blk", "tp"),
            P("grp", "blk", "tp"),
            P("grp", None, "tp"),
        ),
        out_specs=P(("blk", "grp"), "tp"),
        check_vma=False,
    )
```

profile of v0, /device:TPU:0, one launch (start us, length us, event | category | flops | bytes accessed | tf_op | source)
XLA Modules:
  0.0 60.4 jit_solution(226674891747251223)
XLA Ops:
  0.0 1.0 %own_rows.1.first.here.x = bf16[128,1280]{1,0:T(8,128)(2,1)S(1)} custom-call(bf16[256,1280]{1,0:T(8,128)(2,1)} %tokens.4), custom_call_target="tpu_custom_call" | custom-call | bytes 655360 | tf_op jit(solution)/shard_map/own_rows/pallas_call | solution.py:58
  1.0 3.1 %collective-permute-start.1 = (bf16[128,1280]{1,0:T(8,128)(2,1)S(1)}, bf16[128,1280]{1,0:T(8,128)(2,1)S(1)}, u32[]{:S(2)}, u32[]{:S(2)}) collective-permute-start(bf16[128,1280]{1,0:T(8,128)(2,1)S(1)} %own_rows.1.first.here.x), channel_id=1, source_target_pairs={{0,1},{1,2},{2,3},{3,0},{4,5},{5,6},{6,7},{7,4},{8,9},{9,10},{10,1... | collective-permute-start | bytes 983048 | tf_op jit(solution)/shard_map/ppermute | solution.py:164
  4.1 2.1 %collective-permute-start.2 = (bf16[128,1280]{1,0:T(8,128)(2,1)S(1)}, bf16[128,1280]{1,0:T(8,128)(2,1)S(1)}, u32[]{:S(2)}, u32[]{:S(2)}) collective-permute-start(bf16[128,1280]{1,0:T(8,128)(2,1)S(1)} %own_rows.1.first.here.x), channel_id=1, source_target_pairs={{0,3},{1,0},{2,1},{3,2},{4,7},{5,4},{6,5},{7,6},{8,11},{9,8},{10,9... | collective-permute-start | bytes 983048 | tf_op jit(solution)/shard_map/ppermute | solution.py:165
  6.2 1.3 %other_rows_and_weights.1 = (bf16[128,1280]{1,0:T(8,128)(2,1)S(1)}, bf16[384,1280]{1,0:T(8,128)(2,1)S(1)}) custom-call(bf16[256,1280]{1,0:T(8,128)(2,1)} %tokens.4, bf16[192,1280]{1,0:T(8,128)(2,1)} %bitcast.12, bf16[192,1280]{1,0:T(8,128)(2,1)} %bitcast.13, bf16[128,1280]{1,0:T(8,128)(2,1)S(1)} %own_rows.1.first.here.x), custom_call_target="tpu_custom_call" | custom-call | bytes 3276800 | tf_op jit(solution)/shard_map/other_rows_and_weights/pallas_call | solution.py:68
  7.5 1.7 %collective-permute-start = (bf16[384,1280]{1,0:T(8,128)(2,1)S(1)}, bf16[384,1280]{1,0:T(8,128)(2,1)S(1)}, u32[]{:S(2)}, u32[]{:S(2)}) collective-permute-start(bf16[384,1280]{1,0:T(8,128)(2,1)S(1)} %get-tuple-element.14.refs_0_), channel_id=1, source_target_pairs={{0,16},{8,24},{16,0},{24,8},{1,17},{9,25},{17,1},{25,9},{2,18},{10... | collective-permute-start | bytes 2949128 | tf_op jit(solution)/shard_map/ppermute | solution.py:151
  9.2 0.7 %collective-permute-start.6 = (bf16[128,1280]{1,0:T(8,128)(2,1)S(1)}, bf16[128,1280]{1,0:T(8,128)(2,1)S(1)}, u32[]{:S(2)}, u32[]{:S(2)}) collective-permute-start(bf16[128,1280]{1,0:T(8,128)(2,1)S(1)} %get-tuple-element.15.here), channel_id=1, source_target_pairs={{0,5},{1,6},{2,7},{3,4},{4,1},{5,2},{6,3},{7,0},{8,13},{9,14},{10,... | collective-permute-start | bytes 983048 | tf_op jit(solution)/shard_map/ppermute | solution.py:164
  9.9 4.0 %collective-permute-start.7 = (bf16[128,1280]{1,0:T(8,128)(2,1)S(1)}, bf16[128,1280]{1,0:T(8,128)(2,1)S(1)}, u32[]{:S(2)}, u32[]{:S(2)}) collective-permute-start(bf16[128,1280]{1,0:T(8,128)(2,1)S(1)} %get-tuple-element.15.here), channel_id=1, source_target_pairs={{0,7},{1,4},{2,5},{3,6},{4,3},{5,0},{6,1},{7,2},{8,15},{9,12},{10,... | collective-permute-start | bytes 983048 | tf_op jit(solution)/shard_map/ppermute | solution.py:165
  13.9 0.7 %copy-done.1 = bf16[256]{0:T(256)(128)(2,1)S(1)} copy-done((bf16[256]{0:T(256)(128)(2,1)S(1)}, bf16[256]{0:T(256)(128)(2,1)}, u32[]{:S(2)}) %copy-start.1) | copy-done | bytes 536
  14.6 0.7 %copy-done.2 = s32[2]{0:T(128)S(1)} copy-done((s32[2]{0:T(128)S(1)}, s32[2]{0:T(128)}, u32[]{:S(2)}) %copy-start.2) | copy-done | bytes 32
  15.2 0.6 weigh.1.scales
  15.8 0.0 collective-permute-done.1.right
  15.8 10.0 %collective-permute-done.2.left = bf16[128,1280]{1,0:T(8,128)(2,1)S(1)} collective-permute-done((bf16[128,1280]{1,0:T(8,128)(2,1)S(1)}, bf16[128,1280]{1,0:T(8,128)(2,1)S(1)}, u32[]{:S(2)}, u32[]{:S(2)}) %collective-permute-start.2) | collective-permute-done | bytes 327712 | tf_op jit(solution)/shard_map/ppermute | solution.py:165
  25.9 0.1 choose.2
  26.0 0.1 collective-permute-start.5
  26.0 1.0 %attach_weights.1 = bf16[144,1280]{1,0:T(8,128)(2,1)S(1)} custom-call(bf16[256,1280]{1,0:T(8,128)(2,1)} %tokens.4, f32[2,128]{1,0:T(2,128)S(1)} %weigh.1.scales), custom_call_target="tpu_custom_call" | custom-call | bytes 655360 | tf_op jit(solution)/shard_map/attach_weights/pallas_call | solution.py:118
  27.0 0.5 collective-permute-start.8
  27.5 3.2 %collective-permute-done.refs_2_ = bf16[384,1280]{1,0:T(8,128)(2,1)S(1)} collective-permute-done((bf16[384,1280]{1,0:T(8,128)(2,1)S(1)}, bf16[384,1280]{1,0:T(8,128)(2,1)S(1)}, u32[]{:S(2)}, u32[]{:S(2)}) %collective-permute-start) | collective-permute-done | bytes 983072 | tf_op jit(solution)/shard_map/ppermute | solution.py:151
  30.7 0.0 collective-permute-start.4
  30.8 0.0 collective-permute-done.6.refs_0_.right
  30.8 0.5 collective-permute-start.3
  31.3 4.7 %collective-permute-done.7.refs_1_.left = bf16[128,1280]{1,0:T(8,128)(2,1)S(1)} collective-permute-done((bf16[128,1280]{1,0:T(8,128)(2,1)S(1)}, bf16[128,1280]{1,0:T(8,128)(2,1)S(1)}, u32[]{:S(2)}, u32[]{:S(2)}) %collective-permute-start.7) | collective-permute-done | bytes 327712 | tf_op jit(solution)/shard_map/ppermute | solution.py:165
  36.0 0.1 choose.3
  36.1 1.5 %collective-permute-start.9 = (bf16[128,1280]{1,0:T(8,128)(2,1)S(1)}, bf16[128,1280]{1,0:T(8,128)(2,1)S(1)}, u32[]{:S(2)}, u32[]{:S(2)}) collective-permute-start(bf16[128,1280]{1,0:T(8,128)(2,1)S(1)} %choose.3), channel_id=1, source_target_pairs={{0,6},{3,5},{2,3},{1,0},{4,2},{7,1},{6,7},{5,4},{8,14},{11,13},{10... | collective-permute-start | bytes 983048 | tf_op jit(solution)/shard_map/ppermute | solution.py:188
  37.6 0.0 collective-permute-done.3.refs_1_
  37.6 0.0 collective-permute-done.4.refs_3_
  37.6 1.3 %weights_in_order.1.panel = bf16[4,384,1280]{2,1,0:T(8,128)(2,1)S(1)} custom-call(bf16[384,1280]{1,0:T(8,128)(2,1)S(1)} %get-tuple-element.14.refs_0_, bf16[384,1280]{1,0:T(8,128)(2,1)S(1)} %collective-permute-done.3.refs_1_, bf16[384,1280]{1,0:T(8,128)(2,1)S(1)} %collective-permute-done.refs_2_, bf16[384,1280]{1,0:T(8,128)(2,1)S(1)} %collective-permute-done.4.refs_3_), custom_call_target="tpu_custom_call" | custom-call | bytes 7864320 | tf_op jit(solution)/shard_map/weights_in_order/pallas_call | solution.py:138
  38.9 0.0 copy-start
  38.9 3.2 %collective-permute-done.5.opposite = bf16[128,1280]{1,0:T(8,128)(2,1)S(1)} collective-permute-done((bf16[128,1280]{1,0:T(8,128)(2,1)S(1)}, bf16[128,1280]{1,0:T(8,128)(2,1)S(1)}, u32[]{:S(2)}, u32[]{:S(2)}) %collective-permute-start.5) | collective-permute-done | bytes 327712 | tf_op jit(solution)/shard_map/ppermute | solution.py:188
  42.1 1.7 %hidden_rows.1 = (bf16[192,128]{1,0:T(8,128)(2,1)S(1)}, f32[384,128]{1,0:T(8,128)S(1)}) custom-call(bf16[4,384,1280]{2,1,0:T(8,128)(2,1)S(1)} %weights_in_order.1.panel, bf16[128,1280]{1,0:T(8,128)(2,1)S(1)} %collective-permute-done.1.right, bf16[128,1280]{1,0:T(8,128)(2,1)S(1)} %collective-permute-done.2.left, bf16[128,1280]{1,0:T(8,128)(2,1)S(1)} %own_rows.1.first.here.x, ...), custom_call_target="tpu_custom_call" | custom-call | flops 503316480 | bytes 3932160 | tf_op jit(solution)/shard_map/hidden_rows/pallas_call | solution.py:231
  43.8 1.6 %collective-permute-start.13 = (bf16[192,128]{1,0:T(8,128)(2,1)S(1)}, bf16[192,128]{1,0:T(8,128)(2,1)S(1)}, u32[]{:S(2)}, u32[]{:S(2)}) collective-permute-start(bf16[192,128]{1,0:T(8,128)(2,1)S(1)} %get-tuple-element.18.refs_0_), channel_id=1, source_target_pairs={{0,1},{1,2},{2,3},{3,0},{4,5},{5,6},{6,7},{7,4},{8,9},{9,10},{10,1... | collective-permute-start | bytes 147464 | tf_op jit(solution)/shard_map/ppermute | solution.py:308
  45.3 2.3 %collective-permute-start.14 = (bf16[192,128]{1,0:T(8,128)(2,1)S(1)}, bf16[192,128]{1,0:T(8,128)(2,1)S(1)}, u32[]{:S(2)}, u32[]{:S(2)}) collective-permute-start(bf16[192,128]{1,0:T(8,128)(2,1)S(1)} %get-tuple-element.18.refs_0_), channel_id=1, source_target_pairs={{0,3},{1,0},{2,1},{3,2},{4,7},{5,4},{6,5},{7,6},{8,11},{9,8},{10,9... | collective-permute-start | bytes 147464 | tf_op jit(solution)/shard_map/ppermute | solution.py:308
  47.6 0.0 collective-permute-start.15
  47.6 1.7 %collective-permute-done.9.opposite = bf16[128,1280]{1,0:T(8,128)(2,1)S(1)} collective-permute-done((bf16[128,1280]{1,0:T(8,128)(2,1)S(1)}, bf16[128,1280]{1,0:T(8,128)(2,1)S(1)}, u32[]{:S(2)}, u32[]{:S(2)}) %collective-permute-start.9) | collective-permute-done | bytes 327712 | tf_op jit(solution)/shard_map/ppermute | solution.py:188
  49.3 0.0 collective-permute-done.8.x
  49.3 0.7 %last_chunks.1.refs_0_ = bf16[192,128]{1,0:T(8,128)(2,1)S(1)} custom-call(bf16[4,384,1280]{2,1,0:T(8,128)(2,1)S(1)} %weights_in_order.1.panel, f32[384,128]{1,0:T(8,128)S(1)} %get-tuple-element.16.total, bf16[144,1280]{1,0:T(8,128)(2,1)S(1)} %collective-permute-done.8.x, bf16[128,1280]{1,0:T(8,128)(2,1)S(1)} %collective-permute-done.9.opposite), custom_call_target="tpu_custom_call" | custom-call | flops 251658240 | bytes 1966080 | tf_op jit(solution)/shard_map/last_chunks/pallas_call | solution.py:231
  50.0 2.5 %collective-permute-start.11 = (bf16[192,128]{1,0:T(8,128)(2,1)S(1)}, bf16[192,128]{1,0:T(8,128)(2,1)S(1)}, u32[]{:S(2)}, u32[]{:S(2)}) collective-permute-start(bf16[192,128]{1,0:T(8,128)(2,1)S(1)} %last_chunks.1.refs_0_), channel_id=1, source_target_pairs={{0,1},{1,2},{2,3},{3,0},{4,5},{5,6},{6,7},{7,4},{8,9},{9,10},{10,1... | collective-permute-start | bytes 147464 | tf_op jit(solution)/shard_map/ppermute | solution.py:308
  52.5 1.4 %collective-permute-start.12 = (bf16[192,128]{1,0:T(8,128)(2,1)S(1)}, bf16[192,128]{1,0:T(8,128)(2,1)S(1)}, u32[]{:S(2)}, u32[]{:S(2)}) collective-permute-start(bf16[192,128]{1,0:T(8,128)(2,1)S(1)} %last_chunks.1.refs_0_), channel_id=1, source_target_pairs={{0,3},{1,0},{2,1},{3,2},{4,7},{5,4},{6,5},{7,6},{8,11},{9,8},{10,9... | collective-permute-start | bytes 147464 | tf_op jit(solution)/shard_map/ppermute | solution.py:308
  53.9 0.0 collective-permute-done.13.refs_1_
  53.9 0.8 %collective-permute-start.10 = (bf16[192,128]{1,0:T(8,128)(2,1)S(1)}, bf16[192,128]{1,0:T(8,128)(2,1)S(1)}, u32[]{:S(2)}, u32[]{:S(2)}) collective-permute-start(bf16[192,128]{1,0:T(8,128)(2,1)S(1)} %last_chunks.1.refs_0_), channel_id=1, source_target_pairs={{0,2},{1,3},{2,0},{3,1},{4,6},{5,7},{6,4},{7,5},{8,10},{9,11},{10,... | collective-permute-start | bytes 147464 | tf_op jit(solution)/shard_map/ppermute | solution.py:308
  54.7 0.0 collective-permute-done.14.refs_2_
  54.7 0.0 collective-permute-done.15.refs_3_
  54.7 0.0 copy-done
  54.7 1.3 %project_down.2.refs_3_ = bf16[256,1280]{1,0:T(8,128)(2,1)} custom-call(bf16[192,128]{1,0:T(8,128)(2,1)S(1)} %get-tuple-element.18.refs_0_, bf16[192,128]{1,0:T(8,128)(2,1)S(1)} %collective-permute-done.13.refs_1_, bf16[192,128]{1,0:T(8,128)(2,1)S(1)} %collective-permute-done.14.refs_2_, bf16[192,128]{1,0:T(8,128)(2,1)S(1)} %collective-permute-done.15.refs_3_, ...), custom_call_target="tpu_custom_call" | custom-call | flops 8000000000 | bytes 2293760 | tf_op jit(solution)/shard_map/project_down/pallas_call | solution.py:294
  56.0 0.0 collective-permute-done.11.refs_1_
  56.0 0.9 %collective-permute-done.12.refs_2_ = bf16[192,128]{1,0:T(8,128)(2,1)S(1)} collective-permute-done((bf16[192,128]{1,0:T(8,128)(2,1)S(1)}, bf16[192,128]{1,0:T(8,128)(2,1)S(1)}, u32[]{:S(2)}, u32[]{:S(2)}) %collective-permute-start.12) | collective-permute-done | bytes 49184 | tf_op jit(solution)/shard_map/ppermute | solution.py:308
  56.9 0.5 early_down.1.refs_2_
  57.4 2.0 %collective-permute-done.10.refs_0_ = bf16[192,128]{1,0:T(8,128)(2,1)S(1)} collective-permute-done((bf16[192,128]{1,0:T(8,128)(2,1)S(1)}, bf16[192,128]{1,0:T(8,128)(2,1)S(1)}, u32[]{:S(2)}, u32[]{:S(2)}) %collective-permute-start.10) | collective-permute-done | bytes 49184 | tf_op jit(solution)/shard_map/ppermute | solution.py:308
  59.4 1.0 %project_down.3 = bf16[256,1280]{1,0:T(8,128)(2,1)} custom-call(bf16[192,128]{1,0:T(8,128)(2,1)S(1)} %collective-permute-done.10.refs_0_, bf16[768,1280]{1,0:T(8,128)(2,1)S(1)} %bitcast.10, f32[128,1280]{1,0:T(8,128)S(1)} %early_down.1.refs_2_, bf16[256,1280]{1,0:T(8,128)(2,1)} %project_down.2.refs_3_), custom_call_target="tpu_custom_call", output_to_operand_aliasing={{}: (3, {})} | custom-call | flops 125829120 | bytes 2293760 | tf_op jit(solution)/shard_map/project_down/pallas_call | solution.py:294
  (2 shorter events, 0.0 us)
Async XLA Ops:
  1.0 14.8 %collective-permute-start.1 = (bf16[128,1280]{1,0:T(8,128)(2,1)S(1)}, bf16[128,1280]{1,0:T(8,128)(2,1)S(1)}, u32[]{:S(2)}, u32[]{:S(2)}) collective-permute-start(bf16[128,1280]{1,0:T(8,128)(2,1)S(1)} %own_rows.1.first.here.x), channel_id=1, source_target_pairs={{0,1},{1,2},{2,3},{3,0},{4,5},{5,6},{6,7},{7,4},{8,9},{9,10},{10,1... | collective-permute-start | bytes 983048 | tf_op jit(solution)/shard_map/ppermute | solution.py:164
  4.1 21.8 %collective-permute-start.2 = (bf16[128,1280]{1,0:T(8,128)(2,1)S(1)}, bf16[128,1280]{1,0:T(8,128)(2,1)S(1)}, u32[]{:S(2)}, u32[]{:S(2)}) collective-permute-start(bf16[128,1280]{1,0:T(8,128)(2,1)S(1)} %own_rows.1.first.here.x), channel_id=1, source_target_pairs={{0,3},{1,0},{2,1},{3,2},{4,7},{5,4},{6,5},{7,6},{8,11},{9,8},{10,9... | collective-permute-start | bytes 983048 | tf_op jit(solution)/shard_map/ppermute | solution.py:165
  7.5 23.3 %collective-permute-start = (bf16[384,1280]{1,0:T(8,128)(2,1)S(1)}, bf16[384,1280]{1,0:T(8,128)(2,1)S(1)}, u32[]{:S(2)}, u32[]{:S(2)}) collective-permute-start(bf16[384,1280]{1,0:T(8,128)(2,1)S(1)} %get-tuple-element.14.refs_0_), channel_id=1, source_target_pairs={{0,16},{8,24},{16,0},{24,8},{1,17},{9,25},{17,1},{25,9},{2,18},{10... | collective-permute-start | bytes 2949128 | tf_op jit(solution)/shard_map/ppermute | solution.py:151
  9.2 21.5 %collective-permute-start.6 = (bf16[128,1280]{1,0:T(8,128)(2,1)S(1)}, bf16[128,1280]{1,0:T(8,128)(2,1)S(1)}, u32[]{:S(2)}, u32[]{:S(2)}) collective-permute-start(bf16[128,1280]{1,0:T(8,128)(2,1)S(1)} %get-tuple-element.15.here), channel_id=1, source_target_pairs={{0,5},{1,6},{2,7},{3,4},{4,1},{5,2},{6,3},{7,0},{8,13},{9,14},{10,... | collective-permute-start | bytes 983048 | tf_op jit(solution)/shard_map/ppermute | solution.py:164
  9.9 26.1 %collective-permute-start.7 = (bf16[128,1280]{1,0:T(8,128)(2,1)S(1)}, bf16[128,1280]{1,0:T(8,128)(2,1)S(1)}, u32[]{:S(2)}, u32[]{:S(2)}) collective-permute-start(bf16[128,1280]{1,0:T(8,128)(2,1)S(1)} %get-tuple-element.15.here), channel_id=1, source_target_pairs={{0,7},{1,4},{2,5},{3,6},{4,3},{5,0},{6,1},{7,2},{8,15},{9,12},{10,... | collective-permute-start | bytes 983048 | tf_op jit(solution)/shard_map/ppermute | solution.py:165
  13.9 0.7 %copy-start.1 = (bf16[256]{0:T(256)(128)(2,1)S(1)}, bf16[256]{0:T(256)(128)(2,1)}, u32[]{:S(2)}) copy-start(bf16[256]{0:T(256)(128)(2,1)} %param.7) | copy-start | bytes 1540
  14.6 0.7 %copy-start.2 = (s32[2]{0:T(128)S(1)}, s32[2]{0:T(128)}, u32[]{:S(2)}) copy-start(s32[2]{0:T(128)} %counts.1) | copy-start | bytes 28
  26.0 16.1 %collective-permute-start.5 = (bf16[128,1280]{1,0:T(8,128)(2,1)S(1)}, bf16[128,1280]{1,0:T(8,128)(2,1)S(1)}, u32[]{:S(2)}, u32[]{:S(2)}) collective-permute-start(bf16[128,1280]{1,0:T(8,128)(2,1)S(1)} %choose.2), channel_id=1, source_target_pairs={{0,2},{3,1},{2,3},{1,0},{4,6},{7,5},{6,7},{5,4},{8,10},{11,9},{10,... | collective-permute-start | bytes 983048 | tf_op jit(solution)/shard_map/ppermute | solution.py:188
  27.0 22.3 %collective-permute-start.8 = (bf16[144,1280]{1,0:T(8,128)(2,1)S(1)}, bf16[144,1280]{1,0:T(8,128)(2,1)S(1)}, u32[]{:S(2)}, u32[]{:S(2)}) collective-permute-start(bf16[144,1280]{1,0:T(8,128)(2,1)S(1)} %attach_weights.1), channel_id=1, source_target_pairs={{0,4},{4,0},{1,5},{5,1},{2,6},{6,2},{3,7},{7,3},{8,12},{12,8},{9,1... | collective-permute-start | bytes 1105928 | tf_op jit(solution)/shard_map/ppermute | solution.py:323
  30.7 6.9 %collective-permute-start.4 = (bf16[384,1280]{1,0:T(8,128)(2,1)S(1)}, bf16[384,1280]{1,0:T(8,128)(2,1)S(1)}, u32[]{:S(2)}, u32[]{:S(2)}) collective-permute-start(bf16[384,1280]{1,0:T(8,128)(2,1)S(1)} %collective-permute-done.refs_2_), channel_id=1, source_target_pairs={{0,8},{8,0},{16,24},{24,16},{1,9},{9,1},{17,25},{25,17},{2,10},{10... | collective-permute-start | bytes 2949128 | tf_op jit(solution)/shard_map/ppermute | solution.py:151
  30.8 6.9 %collective-permute-start.3 = (bf16[384,1280]{1,0:T(8,128)(2,1)S(1)}, bf16[384,1280]{1,0:T(8,128)(2,1)S(1)}, u32[]{:S(2)}, u32[]{:S(2)}) collective-permute-start(bf16[384,1280]{1,0:T(8,128)(2,1)S(1)} %get-tuple-element.14.refs_0_), channel_id=1, source_target_pairs={{0,8},{8,0},{16,24},{24,16},{1,9},{9,1},{17,25},{25,17},{2,10},{10... | collective-permute-start | bytes 2949128 | tf_op jit(solution)/shard_map/ppermute | solution.py:151
  36.1 13.2 %collective-permute-start.9 = (bf16[128,1280]{1,0:T(8,128)(2,1)S(1)}, bf16[128,1280]{1,0:T(8,128)(2,1)S(1)}, u32[]{:S(2)}, u32[]{:S(2)}) collective-permute-start(bf16[128,1280]{1,0:T(8,128)(2,1)S(1)} %choose.3), channel_id=1, source_target_pairs={{0,6},{3,5},{2,3},{1,0},{4,2},{7,1},{6,7},{5,4},{8,14},{11,13},{10... | collective-permute-start | bytes 983048 | tf_op jit(solution)/shard_map/ppermute | solution.py:188
  38.9 15.8 %copy-start = (bf16[1,768,1280]{2,1,0:T(8,128)(2,1)S(1)}, bf16[1,768,1280]{2,1,0:T(8,128)(2,1)}, u32[]{:S(2)}) copy-start(bf16[1,768,1280]{2,1,0:T(8,128)(2,1)} %param.11) | copy-start | bytes 5898244
  43.8 10.1 %collective-permute-start.13 = (bf16[192,128]{1,0:T(8,128)(2,1)S(1)}, bf16[192,128]{1,0:T(8,128)(2,1)S(1)}, u32[]{:S(2)}, u32[]{:S(2)}) collective-permute-start(bf16[192,128]{1,0:T(8,128)(2,1)S(1)} %get-tuple-element.18.refs_0_), channel_id=1, source_target_pairs={{0,1},{1,2},{2,3},{3,0},{4,5},{5,6},{6,7},{7,4},{8,9},{9,10},{10,1... | collective-permute-start | bytes 147464 | tf_op jit(solution)/shard_map/ppermute | solution.py:308
  45.3 9.4 %collective-permute-start.14 = (bf16[192,128]{1,0:T(8,128)(2,1)S(1)}, bf16[192,128]{1,0:T(8,128)(2,1)S(1)}, u32[]{:S(2)}, u32[]{:S(2)}) collective-permute-start(bf16[192,128]{1,0:T(8,128)(2,1)S(1)} %get-tuple-element.18.refs_0_), channel_id=1, source_target_pairs={{0,3},{1,0},{2,1},{3,2},{4,7},{5,4},{6,5},{7,6},{8,11},{9,8},{10,9... | collective-permute-start | bytes 147464 | tf_op jit(solution)/shard_map/ppermute | solution.py:308
  47.6 7.1 %collective-permute-start.15 = (bf16[192,128]{1,0:T(8,128)(2,1)S(1)}, bf16[192,128]{1,0:T(8,128)(2,1)S(1)}, u32[]{:S(2)}, u32[]{:S(2)}) collective-permute-start(bf16[192,128]{1,0:T(8,128)(2,1)S(1)} %get-tuple-element.18.refs_0_), channel_id=1, source_target_pairs={{0,2},{1,3},{2,0},{3,1},{4,6},{5,7},{6,4},{7,5},{8,10},{9,11},{10,... | collective-permute-start | bytes 147464 | tf_op jit(solution)/shard_map/ppermute | solution.py:308
  50.0 6.0 %collective-permute-start.11 = (bf16[192,128]{1,0:T(8,128)(2,1)S(1)}, bf16[192,128]{1,0:T(8,128)(2,1)S(1)}, u32[]{:S(2)}, u32[]{:S(2)}) collective-permute-start(bf16[192,128]{1,0:T(8,128)(2,1)S(1)} %last_chunks.1.refs_0_), channel_id=1, source_target_pairs={{0,1},{1,2},{2,3},{3,0},{4,5},{5,6},{6,7},{7,4},{8,9},{9,10},{10,1... | collective-permute-start | bytes 147464 | tf_op jit(solution)/shard_map/ppermute | solution.py:308
  52.5 4.5 %collective-permute-start.12 = (bf16[192,128]{1,0:T(8,128)(2,1)S(1)}, bf16[192,128]{1,0:T(8,128)(2,1)S(1)}, u32[]{:S(2)}, u32[]{:S(2)}) collective-permute-start(bf16[192,128]{1,0:T(8,128)(2,1)S(1)} %last_chunks.1.refs_0_), channel_id=1, source_target_pairs={{0,3},{1,0},{2,1},{3,2},{4,7},{5,4},{6,5},{7,6},{8,11},{9,8},{10,9... | collective-permute-start | bytes 147464 | tf_op jit(solution)/shard_map/ppermute | solution.py:308
  53.9 5.5 %collective-permute-start.10 = (bf16[192,128]{1,0:T(8,128)(2,1)S(1)}, bf16[192,128]{1,0:T(8,128)(2,1)S(1)}, u32[]{:S(2)}, u32[]{:S(2)}) collective-permute-start(bf16[192,128]{1,0:T(8,128)(2,1)S(1)} %last_chunks.1.refs_0_), channel_id=1, source_target_pairs={{0,2},{1,3},{2,0},{3,1},{4,6},{5,7},{6,4},{7,5},{8,10},{9,11},{10,... | collective-permute-start | bytes 147464 | tf_op jit(solution)/shard_map/ppermute | solution.py:308
where the time goes:
time: 60.6 us; the launch traced here: 60.4 us
  waiting for transfers between devices  25.8 us (43%)
  starting transfers between devices  22.8 us (38%)
  Pallas kernels  10.4 us (17%)
  local copies, waits for them, and re-layouts  1.32 us (2%)
    ppermute x2, waiting for transfers between devices, ring(): lax.ppermute(block, ('grp', 'tp'), along(step, [(i, (i + 3) % 4) for i in...  14.8 us
    ppermute x6, starting transfers between devices, everywhere(): lax.ppermute(hidden, 'tp', [(i, (i + s) % 4) for i in range(4)])  8.57 us
    ppermute x2, starting transfers between devices, ring(): lax.ppermute(block, ('grp', 'tp'), along(step, [(i, (i + 3) % 4) for i in...  6.11 us
    ppermute x2, waiting for transfers between devices, middle(): lax.ppermute(block, ('grp', 'tp'), along(step, [(0, 2), (3, 1)], [(2, 3),...  4.85 us
    ppermute x2, starting transfers between devices, ring(): lax.ppermute(block, ('grp', 'tp'), along(step, [(i, (i + 1) % 4) for i in...  3.78 us
    ppermute x3, waiting for transfers between devices, swap(): lax.ppermute(x, axis, [(i, i ^ bit) for i in range(lax.axis_size(axis))])  3.24 us
    ppermute x6, waiting for transfers between devices, everywhere(): lax.ppermute(hidden, 'tp', [(i, (i + s) % 4) for i in range(4)])  2.94 us
    pallas_call x2, Pallas kernels, call_rows(): pl.pallas_call(kernel, out_shape=outs, in_specs=[VMEM] * (1 + len(operand...  2.35 us
  transfers between devices with their start and end apart: 16, of which 7 were waited for; matrix products, arithmetic and copies ran while one was open for 0% of the time, Pallas kernels for 14%

commit v1 on v0

--- a/solution.py
+++ b/solution.py
@@ -11,9 +11,9 @@
 VMEM = pl.BlockSpec(memory_space=pltpu.VMEM)
 WHOLE = pl.BlockSpec(memory_space=pl.ANY)
 DMA = pltpu.SemaphoreType.DMA
-AHEAD = 3
+AHEAD = 2
 EXTRA = 16
-DISTANCES = (0, 1, 3, 2)
+PLACES = (0, 3, 2, 1)
 
 
 def cost(flops, values, exps=0):
@@ -239,27 +239,27 @@
     )(panel, *operands)
 
 
-def down_sum(hiddens, distances, down):
+def down_sum(hiddens, places, down):
     place = lax.axis_index("tp")
     hid = hiddens[0].shape[0]
     total = 0
-    for hidden, s in zip(hiddens, distances):
-        part = down[rows_at(lax.rem(place - s + 4, 4), hid), :]
+    for hidden, bits in zip(hiddens, places):
+        part = down[rows_at(place ^ bits, hid), :]
         total += lax.dot_general(hidden[...], part, (((0,), (0,)), ((), ())), preferred_element_type=jnp.float32)
     return total
 
 
-def early_kernel(distances, *refs):
-    refs[-1][...] = down_sum(refs[:-2], distances, refs[-2])
-
-
-def down_kernel(step, groups, distances, *refs):
-    count = len(distances)
+def early_kernel(places, *refs):
+    refs[-1][...] = down_sum(refs[:-2], places, refs[-2])
+
+
+def down_kernel(step, groups, places, *refs):
+    count = len(places)
     hiddens, down = refs[:count], refs[count]
     out, rows_here, sem = refs[-3:]
     group = lax.axis_index("grp")
     rows = hiddens[0].shape[1]
-    total = down_sum(hiddens, distances, down)
+    total = down_sum(hiddens, places, down)
     if count < 4:
         total += refs[count + 1][...]
     rows_here[...] = total.astype(rows_here.dtype)
@@ -269,10 +269,10 @@
     copy.wait()
 
 
-def early_sum(hiddens, distances, down):
+def early_sum(hiddens, places, down):
     rows, wide = hiddens[0].shape[1], down.shape[1]
     return pl.pallas_call(
-        functools.partial(early_kernel, distances),
+        functools.partial(early_kernel, places),
         out_shape=jax.ShapeDtypeStruct((rows, wide), jnp.float32),
         in_specs=[VMEM] * (len(hiddens) + 1),
         out_specs=VMEM,
@@ -284,15 +284,15 @@
 
 def project_down(step, groups, hiddens, down, out, ahead):
     rows, wide = hiddens[0].shape[1], down.shape[1]
-    distances = DISTANCES
+    places = PLACES
     earlier = [] if out is None else [out]
     sums = []
     if ahead:
-        sums = [early_sum(hiddens[:ahead], distances[:ahead], down)]
-        hiddens, distances = hiddens[ahead:], distances[ahead:]
+        sums = [early_sum(hiddens[:ahead], places[:ahead], down)]
+        hiddens, places = hiddens[ahead:], places[ahead:]
     count = len(hiddens)
     return pl.pallas_call(
-        functools.partial(down_kernel, step, groups, distances),
+        functools.partial(down_kernel, step, groups, places),
         out_shape=jax.ShapeDtypeStruct((groups * rows, wide), jnp.bfloat16),
         in_specs=[VMEM] * (count + 1 + len(sums)) + [WHOLE] * len(earlier),
         out_specs=WHOLE,
@@ -305,7 +305,7 @@
 
 
 def everywhere(hidden):
-    return [lax.ppermute(hidden, "tp", [(i, (i + s) % 4) for i in range(4)]) if s else hidden for s in DISTANCES]
+    return [swap(hidden, "tp", bits) if bits else hidden for bits in PLACES]
 
 
 def local(dispatched, route_prob, peer_rows, gate_weight, up_weight, down_weight):

time: 60.6 us -> 59.6 us (0.983)
  waiting for transfers between devices: 25.8 us -> 24.5 us
    ppermute x3 -> x9, starting transfers between devices: 2.25 us -> 11.2 us  [swap(): lax.ppermute(x, axis, [(i, i ^ bit) for i in range(lax.axis_size(axis))])]
    ppermute x6 -> x0, starting transfers between devices: 8.57 us -> none  [everywhere(): lax.ppermute(hidden, 'tp', [(i, (i + s) % 4) for i in range(4)])]
    ppermute x6 -> x0, waiting for transfers between devices: 2.94 us -> none  [everywhere(): lax.ppermute(hidden, 'tp', [(i, (i + s) % 4) for i in range(4)])]
    ppermute x3 -> x9, waiting for transfers between devices: 3.24 us -> 5.42 us  [swap(): lax.ppermute(x, axis, [(i, i ^ bit) for i in range(lax.axis_size(axis))])]
  transfers between devices with their start and end apart: 16 -> 16, of which waited for: 7 -> 8; matrix products, arithmetic and copies ran while one was open for 0% -> 0% of each run, Pallas kernels for 14% -> 14%
where the time goes in v1:
time: 59.6 us; the launch traced here: 59.4 us
  waiting for transfers between devices  24.5 us (41%)
  starting transfers between devices  23.1 us (39%)
  Pallas kernels  10.4 us (17%)
  local copies, waits for them, and re-layouts  1.32 us (2%)
    ppermute x2, waiting for transfers between devices, ring(): lax.ppermute(block, ('grp', 'tp'), along(step, [(i, (i + 3) % 4) for i in...  14.8 us
    ppermute x9, starting transfers between devices, swap(): lax.ppermute(x, axis, [(i, i ^ bit) for i in range(lax.axis_size(axis))])  11.2 us
    ppermute x2, starting transfers between devices, ring(): lax.ppermute(block, ('grp', 'tp'), along(step, [(i, (i + 3) % 4) for i in...  6.11 us
    ppermute x9, waiting for transfers between devices, swap(): lax.ppermute(x, axis, [(i, i ^ bit) for i in range(lax.axis_size(axis))])  5.42 us
    ppermute x2, waiting for transfers between devices, middle(): lax.ppermute(block, ('grp', 'tp'), along(step, [(0, 2), (3, 1)], [(2, 3),...  4.27 us
    ppermute x2, starting transfers between devices, ring(): lax.ppermute(block, ('grp', 'tp'), along(step, [(i, (i + 1) % 4) for i in...  3.78 us
    pallas_call x2, Pallas kernels, project_down(): pl.pallas_call(functools.partial(down_kernel, step, groups, places), out_...  2.36 us
    pallas_call x2, Pallas kernels, call_rows(): pl.pallas_call(kernel, out_shape=outs, in_specs=[VMEM] * (1 + len(operand...  2.35 us
  transfers between devices with their start and end apart: 16, of which 8 were waited for; matrix products, arithmetic and copies ran while one was open for 0% of the time, Pallas kernels for 14%

profile of v1, /device:TPU:0, one launch (start us, length us, event | category | flops | bytes accessed | tf_op | source)
XLA Modules:
  0.0 59.4 jit_solution(5922821197587715782)
XLA Ops:
  0.0 1.0 %own_rows.1.first.here.x = bf16[128,1280]{1,0:T(8,128)(2,1)S(1)} custom-call(bf16[256,1280]{1,0:T(8,128)(2,1)} %tokens.4), custom_call_target="tpu_custom_call" | custom-call | bytes 655360 | tf_op jit(solution)/shard_map/own_rows/pallas_call | solution.py:58
  1.0 3.1 %collective-permute-start.1 = (bf16[128,1280]{1,0:T(8,128)(2,1)S(1)}, bf16[128,1280]{1,0:T(8,128)(2,1)S(1)}, u32[]{:S(2)}, u32[]{:S(2)}) collective-permute-start(bf16[128,1280]{1,0:T(8,128)(2,1)S(1)} %own_rows.1.first.here.x), channel_id=1, source_target_pairs={{0,1},{1,2},{2,3},{3,0},{4,5},{5,6},{6,7},{7,4},{8,9},{9,10},{10,1... | collective-permute-start | bytes 983048 | tf_op jit(solution)/shard_map/ppermute | solution.py:164
  4.1 2.1 %collective-permute-start.2 = (bf16[128,1280]{1,0:T(8,128)(2,1)S(1)}, bf16[128,1280]{1,0:T(8,128)(2,1)S(1)}, u32[]{:S(2)}, u32[]{:S(2)}) collective-permute-start(bf16[128,1280]{1,0:T(8,128)(2,1)S(1)} %own_rows.1.first.here.x), channel_id=1, source_target_pairs={{0,3},{1,0},{2,1},{3,2},{4,7},{5,4},{6,5},{7,6},{8,11},{9,8},{10,9... | collective-permute-start | bytes 983048 | tf_op jit(solution)/shard_map/ppermute | solution.py:165
  6.2 1.3 %other_rows_and_weights.1 = (bf16[128,1280]{1,0:T(8,128)(2,1)S(1)}, bf16[384,1280]{1,0:T(8,128)(2,1)S(1)}) custom-call(bf16[256,1280]{1,0:T(8,128)(2,1)} %tokens.4, bf16[192,1280]{1,0:T(8,128)(2,1)} %bitcast.12, bf16[192,1280]{1,0:T(8,128)(2,1)} %bitcast.13, bf16[128,1280]{1,0:T(8,128)(2,1)S(1)} %own_rows.1.first.here.x), custom_call_target="tpu_custom_call" | custom-call | bytes 3276800 | tf_op jit(solution)/shard_map/other_rows_and_weights/pallas_call | solution.py:68
  7.5 1.7 %collective-permute-start = (bf16[384,1280]{1,0:T(8,128)(2,1)S(1)}, bf16[384,1280]{1,0:T(8,128)(2,1)S(1)}, u32[]{:S(2)}, u32[]{:S(2)}) collective-permute-start(bf16[384,1280]{1,0:T(8,128)(2,1)S(1)} %get-tuple-element.14.refs_0_), channel_id=1, source_target_pairs={{0,16},{8,24},{16,0},{24,8},{1,17},{9,25},{17,1},{25,9},{2,18},{10... | collective-permute-start | bytes 2949128 | tf_op jit(solution)/shard_map/ppermute | solution.py:151
  9.2 0.7 %collective-permute-start.6 = (bf16[128,1280]{1,0:T(8,128)(2,1)S(1)}, bf16[128,1280]{1,0:T(8,128)(2,1)S(1)}, u32[]{:S(2)}, u32[]{:S(2)}) collective-permute-start(bf16[128,1280]{1,0:T(8,128)(2,1)S(1)} %get-tuple-element.15.here), channel_id=1, source_target_pairs={{0,5},{1,6},{2,7},{3,4},{4,1},{5,2},{6,3},{7,0},{8,13},{9,14},{10,... | collective-permute-start | bytes 983048 | tf_op jit(solution)/shard_map/ppermute | solution.py:164
  9.9 4.0 %collective-permute-start.7 = (bf16[128,1280]{1,0:T(8,128)(2,1)S(1)}, bf16[128,1280]{1,0:T(8,128)(2,1)S(1)}, u32[]{:S(2)}, u32[]{:S(2)}) collective-permute-start(bf16[128,1280]{1,0:T(8,128)(2,1)S(1)} %get-tuple-element.15.here), channel_id=1, source_target_pairs={{0,7},{1,4},{2,5},{3,6},{4,3},{5,0},{6,1},{7,2},{8,15},{9,12},{10,... | collective-permute-start | bytes 983048 | tf_op jit(solution)/shard_map/ppermute | solution.py:165
  13.9 0.7 %copy-done.1 = bf16[256]{0:T(256)(128)(2,1)S(1)} copy-done((bf16[256]{0:T(256)(128)(2,1)S(1)}, bf16[256]{0:T(256)(128)(2,1)}, u32[]{:S(2)}) %copy-start.1) | copy-done | bytes 536
  14.6 0.7 %copy-done.2 = s32[2]{0:T(128)S(1)} copy-done((s32[2]{0:T(128)S(1)}, s32[2]{0:T(128)}, u32[]{:S(2)}) %copy-start.2) | copy-done | bytes 32
  15.2 0.6 weigh.1.scales
  15.8 0.0 collective-permute-done.1.right
  15.8 10.0 %collective-permute-done.2.left = bf16[128,1280]{1,0:T(8,128)(2,1)S(1)} collective-permute-done((bf16[128,1280]{1,0:T(8,128)(2,1)S(1)}, bf16[128,1280]{1,0:T(8,128)(2,1)S(1)}, u32[]{:S(2)}, u32[]{:S(2)}) %collective-permute-start.2) | collective-permute-done | bytes 327712 | tf_op jit(solution)/shard_map/ppermute | solution.py:165
  25.9 0.1 choose.2
  26.0 0.1 collective-permute-start.5
  26.0 1.0 %attach_weights.1 = bf16[144,1280]{1,0:T(8,128)(2,1)S(1)} custom-call(bf16[256,1280]{1,0:T(8,128)(2,1)} %tokens.4, f32[2,128]{1,0:T(2,128)S(1)} %weigh.1.scales), custom_call_target="tpu_custom_call" | custom-call | bytes 655360 | tf_op jit(solution)/shard_map/attach_weights/pallas_call | solution.py:118
  27.0 0.5 collective-permute-start.8
  27.5 3.2 %collective-permute-done.refs_2_ = bf16[384,1280]{1,0:T(8,128)(2,1)S(1)} collective-permute-done((bf16[384,1280]{1,0:T(8,128)(2,1)S(1)}, bf16[384,1280]{1,0:T(8,128)(2,1)S(1)}, u32[]{:S(2)}, u32[]{:S(2)}) %collective-permute-start) | collective-permute-done | bytes 983072 | tf_op jit(solution)/shard_map/ppermute | solution.py:151
  30.7 0.0 collective-permute-start.4
  30.8 0.0 collective-permute-done.6.refs_0_.right
  30.8 0.5 collective-permute-start.3
  31.3 4.7 %collective-permute-done.7.refs_1_.left = bf16[128,1280]{1,0:T(8,128)(2,1)S(1)} collective-permute-done((bf16[128,1280]{1,0:T(8,128)(2,1)S(1)}, bf16[128,1280]{1,0:T(8,128)(2,1)S(1)}, u32[]{:S(2)}, u32[]{:S(2)}) %collective-permute-start.7) | collective-permute-done | bytes 327712 | tf_op jit(solution)/shard_map/ppermute | solution.py:165
  36.0 0.1 choose.3
  36.1 1.5 %collective-permute-start.9 = (bf16[128,1280]{1,0:T(8,128)(2,1)S(1)}, bf16[128,1280]{1,0:T(8,128)(2,1)S(1)}, u32[]{:S(2)}, u32[]{:S(2)}) collective-permute-start(bf16[128,1280]{1,0:T(8,128)(2,1)S(1)} %choose.3), channel_id=1, source_target_pairs={{0,6},{3,5},{2,3},{1,0},{4,2},{7,1},{6,7},{5,4},{8,14},{11,13},{10... | collective-permute-start | bytes 983048 | tf_op jit(solution)/shard_map/ppermute | solution.py:188
  37.6 0.0 collective-permute-done.3.refs_1_
  37.6 0.0 collective-permute-done.4.refs_3_
  37.6 1.3 %weights_in_order.1.panel = bf16[4,384,1280]{2,1,0:T(8,128)(2,1)S(1)} custom-call(bf16[384,1280]{1,0:T(8,128)(2,1)S(1)} %get-tuple-element.14.refs_0_, bf16[384,1280]{1,0:T(8,128)(2,1)S(1)} %collective-permute-done.3.refs_1_, bf16[384,1280]{1,0:T(8,128)(2,1)S(1)} %collective-permute-done.refs_2_, bf16[384,1280]{1,0:T(8,128)(2,1)S(1)} %collective-permute-done.4.refs_3_), custom_call_target="tpu_custom_call" | custom-call | bytes 7864320 | tf_op jit(solution)/shard_map/weights_in_order/pallas_call | solution.py:138
  38.9 0.0 copy-start
  38.9 3.2 %collective-permute-done.5.opposite = bf16[128,1280]{1,0:T(8,128)(2,1)S(1)} collective-permute-done((bf16[128,1280]{1,0:T(8,128)(2,1)S(1)}, bf16[128,1280]{1,0:T(8,128)(2,1)S(1)}, u32[]{:S(2)}, u32[]{:S(2)}) %collective-permute-start.5) | collective-permute-done | bytes 327712 | tf_op jit(solution)/shard_map/ppermute | solution.py:188
  42.1 1.7 %hidden_rows.1 = (bf16[192,128]{1,0:T(8,128)(2,1)S(1)}, f32[384,128]{1,0:T(8,128)S(1)}) custom-call(bf16[4,384,1280]{2,1,0:T(8,128)(2,1)S(1)} %weights_in_order.1.panel, bf16[128,1280]{1,0:T(8,128)(2,1)S(1)} %collective-permute-done.1.right, bf16[128,1280]{1,0:T(8,128)(2,1)S(1)} %collective-permute-done.2.left, bf16[128,1280]{1,0:T(8,128)(2,1)S(1)} %own_rows.1.first.here.x, ...), custom_call_target="tpu_custom_call" | custom-call | flops 503316480 | bytes 3932160 | tf_op jit(solution)/shard_map/hidden_rows/pallas_call | solution.py:231
  43.8 2.8 %collective-permute-start.13 = (bf16[192,128]{1,0:T(8,128)(2,1)S(1)}, bf16[192,128]{1,0:T(8,128)(2,1)S(1)}, u32[]{:S(2)}, u32[]{:S(2)}) collective-permute-start(bf16[192,128]{1,0:T(8,128)(2,1)S(1)} %get-tuple-element.18.refs_0_), channel_id=1, source_target_pairs={{0,3},{1,2},{2,1},{3,0},{4,7},{5,6},{6,5},{7,4},{8,11},{9,10},{10,... | collective-permute-start | bytes 147464 | tf_op jit(solution)/shard_map/ppermute | solution.py:151
  46.5 0.3 collective-permute-start.14
  46.8 1.4 %collective-permute-start.15 = (bf16[192,128]{1,0:T(8,128)(2,1)S(1)}, bf16[192,128]{1,0:T(8,128)(2,1)S(1)}, u32[]{:S(2)}, u32[]{:S(2)}) collective-permute-start(bf16[192,128]{1,0:T(8,128)(2,1)S(1)} %get-tuple-element.18.refs_0_), channel_id=1, source_target_pairs={{0,1},{1,0},{2,3},{3,2},{4,5},{5,4},{6,7},{7,6},{8,9},{9,8},{10,11... | collective-permute-start | bytes 147464 | tf_op jit(solution)/shard_map/ppermute | solution.py:151
  48.2 1.1 %collective-permute-done.9.opposite = bf16[128,1280]{1,0:T(8,128)(2,1)S(1)} collective-permute-done((bf16[128,1280]{1,0:T(8,128)(2,1)S(1)}, bf16[128,1280]{1,0:T(8,128)(2,1)S(1)}, u32[]{:S(2)}, u32[]{:S(2)}) %collective-permute-start.9) | collective-permute-done | bytes 327712 | tf_op jit(solution)/shard_map/ppermute | solution.py:188
  49.3 0.0 collective-permute-done.8.x
  49.3 0.7 %last_chunks.1.refs_0_ = bf16[192,128]{1,0:T(8,128)(2,1)S(1)} custom-call(bf16[4,384,1280]{2,1,0:T(8,128)(2,1)S(1)} %weights_in_order.1.panel, f32[384,128]{1,0:T(8,128)S(1)} %get-tuple-element.16.total, bf16[144,1280]{1,0:T(8,128)(2,1)S(1)} %collective-permute-done.8.x, bf16[128,1280]{1,0:T(8,128)(2,1)S(1)} %collective-permute-done.9.opposite), custom_call_target="tpu_custom_call" | custom-call | flops 251658240 | bytes 1966080 | tf_op jit(solution)/shard_map/last_chunks/pallas_call | solution.py:231
  50.0 2.4 %collective-permute-start.12 = (bf16[192,128]{1,0:T(8,128)(2,1)S(1)}, bf16[192,128]{1,0:T(8,128)(2,1)S(1)}, u32[]{:S(2)}, u32[]{:S(2)}) collective-permute-start(bf16[192,128]{1,0:T(8,128)(2,1)S(1)} %last_chunks.1.refs_0_), channel_id=1, source_target_pairs={{0,3},{1,2},{2,1},{3,0},{4,7},{5,6},{6,5},{7,4},{8,11},{9,10},{10,... | collective-permute-start | bytes 147464 | tf_op jit(solution)/shard_map/ppermute | solution.py:151
  52.4 1.5 %collective-permute-start.10 = (bf16[192,128]{1,0:T(8,128)(2,1)S(1)}, bf16[192,128]{1,0:T(8,128)(2,1)S(1)}, u32[]{:S(2)}, u32[]{:S(2)}) collective-permute-start(bf16[192,128]{1,0:T(8,128)(2,1)S(1)} %last_chunks.1.refs_0_), channel_id=1, source_target_pairs={{0,2},{1,3},{2,0},{3,1},{4,6},{5,7},{6,4},{7,5},{8,10},{9,11},{10,... | collective-permute-start | bytes 147464 | tf_op jit(solution)/shard_map/ppermute | solution.py:151
  54.0 0.0 collective-permute-done.13.refs_1_
  54.0 0.5 collective-permute-start.11
  54.5 0.0 collective-permute-done.14.refs_2_
  54.5 0.0 collective-permute-done.15.refs_3_
  54.5 0.0 copy-done
  54.5 1.3 %project_down.2.refs_4_ = bf16[256,1280]{1,0:T(8,128)(2,1)} custom-call(bf16[192,128]{1,0:T(8,128)(2,1)S(1)} %get-tuple-element.18.refs_0_, bf16[192,128]{1,0:T(8,128)(2,1)S(1)} %collective-permute-done.13.refs_1_, bf16[192,128]{1,0:T(8,128)(2,1)S(1)} %collective-permute-done.14.refs_2_, bf16[192,128]{1,0:T(8,128)(2,1)S(1)} %collective-permute-done.15.refs_3_, ...), custom_call_target="tpu_custom_call" | custom-call | flops 8000000000 | bytes 2293760 | tf_op jit(solution)/shard_map/project_down/pallas_call | solution.py:294
  55.8 0.6 %collective-permute-done.12.refs_1_ = bf16[192,128]{1,0:T(8,128)(2,1)S(1)} collective-permute-done((bf16[192,128]{1,0:T(8,128)(2,1)S(1)}, bf16[192,128]{1,0:T(8,128)(2,1)S(1)}, u32[]{:S(2)}, u32[]{:S(2)}) %collective-permute-start.12) | collective-permute-done | bytes 49184 | tf_op jit(solution)/shard_map/ppermute | solution.py:151
  56.4 0.4 early_down.1.refs_3_
  56.8 1.3 %collective-permute-done.10.refs_0_ = bf16[192,128]{1,0:T(8,128)(2,1)S(1)} collective-permute-done((bf16[192,128]{1,0:T(8,128)(2,1)S(1)}, bf16[192,128]{1,0:T(8,128)(2,1)S(1)}, u32[]{:S(2)}, u32[]{:S(2)}) %collective-permute-start.10) | collective-permute-done | bytes 49184 | tf_op jit(solution)/shard_map/ppermute | solution.py:151
  58.1 0.2 collective-permute-done.11.refs_1_
  58.3 1.1 %project_down.3 = bf16[256,1280]{1,0:T(8,128)(2,1)} custom-call(bf16[192,128]{1,0:T(8,128)(2,1)S(1)} %collective-permute-done.10.refs_0_, bf16[192,128]{1,0:T(8,128)(2,1)S(1)} %collective-permute-done.11.refs_1_, bf16[768,1280]{1,0:T(8,128)(2,1)S(1)} %bitcast.10, f32[128,1280]{1,0:T(8,128)S(1)} %early_down.1.refs_3_, ...), custom_call_target="tpu_custom_call", output_to_operand_aliasing={{}: (4, {})} | custom-call | flops 125829120 | bytes 2293760 | tf_op jit(solution)/shard_map/project_down/pallas_call | solution.py:294
  (2 shorter events, 0.0 us)
Async XLA Ops:
  1.0 14.8 %collective-permute-start.1 = (bf16[128,1280]{1,0:T(8,128)(2,1)S(1)}, bf16[128,1280]{1,0:T(8,128)(2,1)S(1)}, u32[]{:S(2)}, u32[]{:S(2)}) collective-permute-start(bf16[128,1280]{1,0:T(8,128)(2,1)S(1)} %own_rows.1.first.here.x), channel_id=1, source_target_pairs={{0,1},{1,2},{2,3},{3,0},{4,5},{5,6},{6,7},{7,4},{8,9},{9,10},{10,1... | collective-permute-start | bytes 983048 | tf_op jit(solution)/shard_map/ppermute | solution.py:164
  4.1 21.8 %collective-permute-start.2 = (bf16[128,1280]{1,0:T(8,128)(2,1)S(1)}, bf16[128,1280]{1,0:T(8,128)(2,1)S(1)}, u32[]{:S(2)}, u32[]{:S(2)}) collective-permute-start(bf16[128,1280]{1,0:T(8,128)(2,1)S(1)} %own_rows.1.first.here.x), channel_id=1, source_target_pairs={{0,3},{1,0},{2,1},{3,2},{4,7},{5,4},{6,5},{7,6},{8,11},{9,8},{10,9... | collective-permute-start | bytes 983048 | tf_op jit(solution)/shard_map/ppermute | solution.py:165
  7.5 23.3 %collective-permute-start = (bf16[384,1280]{1,0:T(8,128)(2,1)S(1)}, bf16[384,1280]{1,0:T(8,128)(2,1)S(1)}, u32[]{:S(2)}, u32[]{:S(2)}) collective-permute-start(bf16[384,1280]{1,0:T(8,128)(2,1)S(1)} %get-tuple-element.14.refs_0_), channel_id=1, source_target_pairs={{0,16},{8,24},{16,0},{24,8},{1,17},{9,25},{17,1},{25,9},{2,18},{10... | collective-permute-start | bytes 2949128 | tf_op jit(solution)/shard_map/ppermute | solution.py:151
  9.2 21.5 %collective-permute-start.6 = (bf16[128,1280]{1,0:T(8,128)(2,1)S(1)}, bf16[128,1280]{1,0:T(8,128)(2,1)S(1)}, u32[]{:S(2)}, u32[]{:S(2)}) collective-permute-start(bf16[128,1280]{1,0:T(8,128)(2,1)S(1)} %get-tuple-element.15.here), channel_id=1, source_target_pairs={{0,5},{1,6},{2,7},{3,4},{4,1},{5,2},{6,3},{7,0},{8,13},{9,14},{10,... | collective-permute-start | bytes 983048 | tf_op jit(solution)/shard_map/ppermute | solution.py:164
  9.9 26.1 %collective-permute-start.7 = (bf16[128,1280]{1,0:T(8,128)(2,1)S(1)}, bf16[128,1280]{1,0:T(8,128)(2,1)S(1)}, u32[]{:S(2)}, u32[]{:S(2)}) collective-permute-start(bf16[128,1280]{1,0:T(8,128)(2,1)S(1)} %get-tuple-element.15.here), channel_id=1, source_target_pairs={{0,7},{1,4},{2,5},{3,6},{4,3},{5,0},{6,1},{7,2},{8,15},{9,12},{10,... | collective-permute-start | bytes 983048 | tf_op jit(solution)/shard_map/ppermute | solution.py:165
  13.9 0.7 %copy-start.1 = (bf16[256]{0:T(256)(128)(2,1)S(1)}, bf16[256]{0:T(256)(128)(2,1)}, u32[]{:S(2)}) copy-start(bf16[256]{0:T(256)(128)(2,1)} %param.7) | copy-start | bytes 1540
  14.6 0.7 %copy-start.2 = (s32[2]{0:T(128)S(1)}, s32[2]{0:T(128)}, u32[]{:S(2)}) copy-start(s32[2]{0:T(128)} %counts.1) | copy-start | bytes 28
  26.0 16.1 %collective-permute-start.5 = (bf16[128,1280]{1,0:T(8,128)(2,1)S(1)}, bf16[128,1280]{1,0:T(8,128)(2,1)S(1)}, u32[]{:S(2)}, u32[]{:S(2)}) collective-permute-start(bf16[128,1280]{1,0:T(8,128)(2,1)S(1)} %choose.2), channel_id=1, source_target_pairs={{0,2},{3,1},{2,3},{1,0},{4,6},{7,5},{6,7},{5,4},{8,10},{11,9},{10,... | collective-permute-start | bytes 983048 | tf_op jit(solution)/shard_map/ppermute | solution.py:188
  27.0 22.3 %collective-permute-start.8 = (bf16[144,1280]{1,0:T(8,128)(2,1)S(1)}, bf16[144,1280]{1,0:T(8,128)(2,1)S(1)}, u32[]{:S(2)}, u32[]{:S(2)}) collective-permute-start(bf16[144,1280]{1,0:T(8,128)(2,1)S(1)} %attach_weights.1), channel_id=1, source_target_pairs={{0,4},{4,0},{1,5},{5,1},{2,6},{6,2},{3,7},{7,3},{8,12},{12,8},{9,1... | collective-permute-start | bytes 1105928 | tf_op jit(solution)/shard_map/ppermute | solution.py:323
  30.7 6.9 %collective-permute-start.4 = (bf16[384,1280]{1,0:T(8,128)(2,1)S(1)}, bf16[384,1280]{1,0:T(8,128)(2,1)S(1)}, u32[]{:S(2)}, u32[]{:S(2)}) collective-permute-start(bf16[384,1280]{1,0:T(8,128)(2,1)S(1)} %collective-permute-done.refs_2_), channel_id=1, source_target_pairs={{0,8},{8,0},{16,24},{24,16},{1,9},{9,1},{17,25},{25,17},{2,10},{10... | collective-permute-start | bytes 2949128 | tf_op jit(solution)/shard_map/ppermute | solution.py:151
  30.8 6.9 %collective-permute-start.3 = (bf16[384,1280]{1,0:T(8,128)(2,1)S(1)}, bf16[384,1280]{1,0:T(8,128)(2,1)S(1)}, u32[]{:S(2)}, u32[]{:S(2)}) collective-permute-start(bf16[384,1280]{1,0:T(8,128)(2,1)S(1)} %get-tuple-element.14.refs_0_), channel_id=1, source_target_pairs={{0,8},{8,0},{16,24},{24,16},{1,9},{9,1},{17,25},{25,17},{2,10},{10... | collective-permute-start | bytes 2949128 | tf_op jit(solution)/shard_map/ppermute | solution.py:151
  36.1 13.2 %collective-permute-start.9 = (bf16[128,1280]{1,0:T(8,128)(2,1)S(1)}, bf16[128,1280]{1,0:T(8,128)(2,1)S(1)}, u32[]{:S(2)}, u32[]{:S(2)}) collective-permute-start(bf16[128,1280]{1,0:T(8,128)(2,1)S(1)} %choose.3), channel_id=1, source_target_pairs={{0,6},{3,5},{2,3},{1,0},{4,2},{7,1},{6,7},{5,4},{8,14},{11,13},{10... | collective-permute-start | bytes 983048 | tf_op jit(solution)/shard_map/ppermute | solution.py:188
  38.9 15.6 %copy-start = (bf16[1,768,1280]{2,1,0:T(8,128)(2,1)S(1)}, bf16[1,768,1280]{2,1,0:T(8,128)(2,1)}, u32[]{:S(2)}) copy-start(bf16[1,768,1280]{2,1,0:T(8,128)(2,1)} %param.11) | copy-start | bytes 5898244
  43.8 10.2 %collective-permute-start.13 = (bf16[192,128]{1,0:T(8,128)(2,1)S(1)}, bf16[192,128]{1,0:T(8,128)(2,1)S(1)}, u32[]{:S(2)}, u32[]{:S(2)}) collective-permute-start(bf16[192,128]{1,0:T(8,128)(2,1)S(1)} %get-tuple-element.18.refs_0_), channel_id=1, source_target_pairs={{0,3},{1,2},{2,1},{3,0},{4,7},{5,6},{6,5},{7,4},{8,11},{9,10},{10,... | collective-permute-start | bytes 147464 | tf_op jit(solution)/shard_map/ppermute | solution.py:151
  46.5 7.9 %collective-permute-start.14 = (bf16[192,128]{1,0:T(8,128)(2,1)S(1)}, bf16[192,128]{1,0:T(8,128)(2,1)S(1)}, u32[]{:S(2)}, u32[]{:S(2)}) collective-permute-start(bf16[192,128]{1,0:T(8,128)(2,1)S(1)} %get-tuple-element.18.refs_0_), channel_id=1, source_target_pairs={{0,2},{1,3},{2,0},{3,1},{4,6},{5,7},{6,4},{7,5},{8,10},{9,11},{10,... | collective-permute-start | bytes 147464 | tf_op jit(solution)/shard_map/ppermute | solution.py:151
  46.8 7.7 %collective-permute-start.15 = (bf16[192,128]{1,0:T(8,128)(2,1)S(1)}, bf16[192,128]{1,0:T(8,128)(2,1)S(1)}, u32[]{:S(2)}, u32[]{:S(2)}) collective-permute-start(bf16[192,128]{1,0:T(8,128)(2,1)S(1)} %get-tuple-element.18.refs_0_), channel_id=1, source_target_pairs={{0,1},{1,0},{2,3},{3,2},{4,5},{5,4},{6,7},{7,6},{8,9},{9,8},{10,11... | collective-permute-start | bytes 147464 | tf_op jit(solution)/shard_map/ppermute | solution.py:151
  50.0 6.4 %collective-permute-start.12 = (bf16[192,128]{1,0:T(8,128)(2,1)S(1)}, bf16[192,128]{1,0:T(8,128)(2,1)S(1)}, u32[]{:S(2)}, u32[]{:S(2)}) collective-permute-start(bf16[192,128]{1,0:T(8,128)(2,1)S(1)} %last_chunks.1.refs_0_), channel_id=1, source_target_pairs={{0,3},{1,2},{2,1},{3,0},{4,7},{5,6},{6,5},{7,4},{8,11},{9,10},{10,... | collective-permute-start | bytes 147464 | tf_op jit(solution)/shard_map/ppermute | solution.py:151
  52.4 5.6 %collective-permute-start.10 = (bf16[192,128]{1,0:T(8,128)(2,1)S(1)}, bf16[192,128]{1,0:T(8,128)(2,1)S(1)}, u32[]{:S(2)}, u32[]{:S(2)}) collective-permute-start(bf16[192,128]{1,0:T(8,128)(2,1)S(1)} %last_chunks.1.refs_0_), channel_id=1, source_target_pairs={{0,2},{1,3},{2,0},{3,1},{4,6},{5,7},{6,4},{7,5},{8,10},{9,11},{10,... | collective-permute-start | bytes 147464 | tf_op jit(solution)/shard_map/ppermute | solution.py:151
  54.0 4.3 %collective-permute-start.11 = (bf16[192,128]{1,0:T(8,128)(2,1)S(1)}, bf16[192,128]{1,0:T(8,128)(2,1)S(1)}, u32[]{:S(2)}, u32[]{:S(2)}) collective-permute-start(bf16[192,128]{1,0:T(8,128)(2,1)S(1)} %last_chunks.1.refs_0_), channel_id=1, source_target_pairs={{0,1},{1,0},{2,3},{3,2},{4,5},{5,4},{6,7},{7,6},{8,9},{9,8},{10,11... | collective-permute-start | bytes 147464 | tf_op jit(solution)/shard_map/ppermute | solution.py:151

commit v2 on v1

--- a/solution.py
+++ b/solution.py
@@ -11,7 +11,7 @@
 VMEM = pl.BlockSpec(memory_space=pltpu.VMEM)
 WHOLE = pl.BlockSpec(memory_space=pl.ANY)
 DMA = pltpu.SemaphoreType.DMA
-AHEAD = 2
+AHEAD = 3
 EXTRA = 16
 PLACES = (0, 3, 2, 1)
 

time: 59.6 us -> 59.8 us (level)
  transfers between devices with their start and end apart: 16 -> 16, of which waited for: 8 -> 7; matrix products, arithmetic and copies ran while one was open for 0% -> 0% of each run, Pallas kernels for 14% -> 14%
where the time goes in v2:
time: 59.8 us; the launch traced here: 59.6 us
  waiting for transfers between devices  24.6 us (41%)
  starting transfers between devices  23.1 us (39%)
  Pallas kernels  10.4 us (17%)
  local copies, waits for them, and re-layouts  1.32 us (2%)
    ppermute x2, waiting for transfers between devices, ring(): lax.ppermute(block, ('grp', 'tp'), along(step, [(i, (i + 3) % 4) for i in...  14.8 us
    ppermute x9, starting transfers between devices, swap(): lax.ppermute(x, axis, [(i, i ^ bit) for i in range(lax.axis_size(axis))])  11.2 us
    ppermute x2, starting transfers between devices, ring(): lax.ppermute(block, ('grp', 'tp'), along(step, [(i, (i + 3) % 4) for i in...  6.11 us
    ppermute x9, waiting for transfers between devices, swap(): lax.ppermute(x, axis, [(i, i ^ bit) for i in range(lax.axis_size(axis))])  5.57 us
    ppermute x2, waiting for transfers between devices, middle(): lax.ppermute(block, ('grp', 'tp'), along(step, [(0, 2), (3, 1)], [(2, 3),...  4.27 us
    ppermute x2, starting transfers between devices, ring(): lax.ppermute(block, ('grp', 'tp'), along(step, [(i, (i + 1) % 4) for i in...  3.78 us
    pallas_call x2, Pallas kernels, call_rows(): pl.pallas_call(kernel, out_shape=outs, in_specs=[VMEM] * (1 + len(operand...  2.35 us
    pallas_call x2, Pallas kernels, project_down(): pl.pallas_call(functools.partial(down_kernel, step, groups, places), out_...  2.28 us
  transfers between devices with their start and end apart: 16, of which 7 were waited for; matrix products, arithmetic and copies ran while one was open for 0% of the time, Pallas kernels for 14%

profile of v2, /device:TPU:0, one launch (start us, length us, event | category | flops | bytes accessed | tf_op | source)
XLA Modules:
  0.0 59.6 jit_solution(2456888818982805292)
XLA Ops:
  0.0 1.0 %own_rows.1.first.here.x = bf16[128,1280]{1,0:T(8,128)(2,1)S(1)} custom-call(bf16[256,1280]{1,0:T(8,128)(2,1)} %tokens.4), custom_call_target="tpu_custom_call" | custom-call | bytes 655360 | tf_op jit(solution)/shard_map/own_rows/pallas_call | solution.py:58
  1.0 3.1 %collective-permute-start.1 = (bf16[128,1280]{1,0:T(8,128)(2,1)S(1)}, bf16[128,1280]{1,0:T(8,128)(2,1)S(1)}, u32[]{:S(2)}, u32[]{:S(2)}) collective-permute-start(bf16[128,1280]{1,0:T(8,128)(2,1)S(1)} %own_rows.1.first.here.x), channel_id=1, source_target_pairs={{0,1},{1,2},{2,3},{3,0},{4,5},{5,6},{6,7},{7,4},{8,9},{9,10},{10,1... | collective-permute-start | bytes 983048 | tf_op jit(solution)/shard_map/ppermute | solution.py:164
  4.1 2.1 %collective-permute-start.2 = (bf16[128,1280]{1,0:T(8,128)(2,1)S(1)}, bf16[128,1280]{1,0:T(8,128)(2,1)S(1)}, u32[]{:S(2)}, u32[]{:S(2)}) collective-permute-start(bf16[128,1280]{1,0:T(8,128)(2,1)S(1)} %own_rows.1.first.here.x), channel_id=1, source_target_pairs={{0,3},{1,0},{2,1},{3,2},{4,7},{5,4},{6,5},{7,6},{8,11},{9,8},{10,9... | collective-permute-start | bytes 983048 | tf_op jit(solution)/shard_map/ppermute | solution.py:165
  6.2 1.3 %other_rows_and_weights.1 = (bf16[128,1280]{1,0:T(8,128)(2,1)S(1)}, bf16[384,1280]{1,0:T(8,128)(2,1)S(1)}) custom-call(bf16[256,1280]{1,0:T(8,128)(2,1)} %tokens.4, bf16[192,1280]{1,0:T(8,128)(2,1)} %bitcast.12, bf16[192,1280]{1,0:T(8,128)(2,1)} %bitcast.13, bf16[128,1280]{1,0:T(8,128)(2,1)S(1)} %own_rows.1.first.here.x), custom_call_target="tpu_custom_call" | custom-call | bytes 3276800 | tf_op jit(solution)/shard_map/other_rows_and_weights/pallas_call | solution.py:68
  7.5 1.7 %collective-permute-start = (bf16[384,1280]{1,0:T(8,128)(2,1)S(1)}, bf16[384,1280]{1,0:T(8,128)(2,1)S(1)}, u32[]{:S(2)}, u32[]{:S(2)}) collective-permute-start(bf16[384,1280]{1,0:T(8,128)(2,1)S(1)} %get-tuple-element.14.refs_0_), channel_id=1, source_target_pairs={{0,16},{8,24},{16,0},{24,8},{1,17},{9,25},{17,1},{25,9},{2,18},{10... | collective-permute-start | bytes 2949128 | tf_op jit(solution)/shard_map/ppermute | solution.py:151
  9.2 0.7 %collective-permute-start.6 = (bf16[128,1280]{1,0:T(8,128)(2,1)S(1)}, bf16[128,1280]{1,0:T(8,128)(2,1)S(1)}, u32[]{:S(2)}, u32[]{:S(2)}) collective-permute-start(bf16[128,1280]{1,0:T(8,128)(2,1)S(1)} %get-tuple-element.15.here), channel_id=1, source_target_pairs={{0,5},{1,6},{2,7},{3,4},{4,1},{5,2},{6,3},{7,0},{8,13},{9,14},{10,... | collective-permute-start | bytes 983048 | tf_op jit(solution)/shard_map/ppermute | solution.py:164
  9.9 4.0 %collective-permute-start.7 = (bf16[128,1280]{1,0:T(8,128)(2,1)S(1)}, bf16[128,1280]{1,0:T(8,128)(2,1)S(1)}, u32[]{:S(2)}, u32[]{:S(2)}) collective-permute-start(bf16[128,1280]{1,0:T(8,128)(2,1)S(1)} %get-tuple-element.15.here), channel_id=1, source_target_pairs={{0,7},{1,4},{2,5},{3,6},{4,3},{5,0},{6,1},{7,2},{8,15},{9,12},{10,... | collective-permute-start | bytes 983048 | tf_op jit(solution)/shard_map/ppermute | solution.py:165
  13.9 0.7 %copy-done.1 = bf16[256]{0:T(256)(128)(2,1)S(1)} copy-done((bf16[256]{0:T(256)(128)(2,1)S(1)}, bf16[256]{0:T(256)(128)(2,1)}, u32[]{:S(2)}) %copy-start.1) | copy-done | bytes 536
  14.6 0.7 %copy-done.2 = s32[2]{0:T(128)S(1)} copy-done((s32[2]{0:T(128)S(1)}, s32[2]{0:T(128)}, u32[]{:S(2)}) %copy-start.2) | copy-done | bytes 32
  15.2 0.6 weigh.1.scales
  15.8 0.0 collective-permute-done.1.right
  15.8 10.0 %collective-permute-done.2.left = bf16[128,1280]{1,0:T(8,128)(2,1)S(1)} collective-permute-done((bf16[128,1280]{1,0:T(8,128)(2,1)S(1)}, bf16[128,1280]{1,0:T(8,128)(2,1)S(1)}, u32[]{:S(2)}, u32[]{:S(2)}) %collective-permute-start.2) | collective-permute-done | bytes 327712 | tf_op jit(solution)/shard_map/ppermute | solution.py:165
  25.9 0.1 choose.2
  26.0 0.1 collective-permute-start.5
  26.0 1.0 %attach_weights.1 = bf16[144,1280]{1,0:T(8,128)(2,1)S(1)} custom-call(bf16[256,1280]{1,0:T(8,128)(2,1)} %tokens.4, f32[2,128]{1,0:T(2,128)S(1)} %weigh.1.scales), custom_call_target="tpu_custom_call" | custom-call | bytes 655360 | tf_op jit(solution)/shard_map/attach_weights/pallas_call | solution.py:118
  27.0 0.5 collective-permute-start.8
  27.5 3.2 %collective-permute-done.refs_2_ = bf16[384,1280]{1,0:T(8,128)(2,1)S(1)} collective-permute-done((bf16[384,1280]{1,0:T(8,128)(2,1)S(1)}, bf16[384,1280]{1,0:T(8,128)(2,1)S(1)}, u32[]{:S(2)}, u32[]{:S(2)}) %collective-permute-start) | collective-permute-done | bytes 983072 | tf_op jit(solution)/shard_map/ppermute | solution.py:151
  30.7 0.0 collective-permute-start.4
  30.8 0.0 collective-permute-done.6.refs_0_.right
  30.8 0.5 collective-permute-start.3
  31.3 4.7 %collective-permute-done.7.refs_1_.left = bf16[128,1280]{1,0:T(8,128)(2,1)S(1)} collective-permute-done((bf16[128,1280]{1,0:T(8,128)(2,1)S(1)}, bf16[128,1280]{1,0:T(8,128)(2,1)S(1)}, u32[]{:S(2)}, u32[]{:S(2)}) %collective-permute-start.7) | collective-permute-done | bytes 327712 | tf_op jit(solution)/shard_map/ppermute | solution.py:165
  36.0 0.1 choose.3
  36.1 1.5 %collective-permute-start.9 = (bf16[128,1280]{1,0:T(8,128)(2,1)S(1)}, bf16[128,1280]{1,0:T(8,128)(2,1)S(1)}, u32[]{:S(2)}, u32[]{:S(2)}) collective-permute-start(bf16[128,1280]{1,0:T(8,128)(2,1)S(1)} %choose.3), channel_id=1, source_target_pairs={{0,6},{3,5},{2,3},{1,0},{4,2},{7,1},{6,7},{5,4},{8,14},{11,13},{10... | collective-permute-start | bytes 983048 | tf_op jit(solution)/shard_map/ppermute | solution.py:188
  37.6 0.0 collective-permute-done.3.refs_1_
  37.6 0.0 collective-permute-done.4.refs_3_
  37.6 1.3 %weights_in_order.1.panel = bf16[4,384,1280]{2,1,0:T(8,128)(2,1)S(1)} custom-call(bf16[384,1280]{1,0:T(8,128)(2,1)S(1)} %get-tuple-element.14.refs_0_, bf16[384,1280]{1,0:T(8,128)(2,1)S(1)} %collective-permute-done.3.refs_1_, bf16[384,1280]{1,0:T(8,128)(2,1)S(1)} %collective-permute-done.refs_2_, bf16[384,1280]{1,0:T(8,128)(2,1)S(1)} %collective-permute-done.4.refs_3_), custom_call_target="tpu_custom_call" | custom-call | bytes 7864320 | tf_op jit(solution)/shard_map/weights_in_order/pallas_call | solution.py:138
  38.9 0.0 copy-start
  38.9 3.2 %collective-permute-done.5.opposite = bf16[128,1280]{1,0:T(8,128)(2,1)S(1)} collective-permute-done((bf16[128,1280]{1,0:T(8,128)(2,1)S(1)}, bf16[128,1280]{1,0:T(8,128)(2,1)S(1)}, u32[]{:S(2)}, u32[]{:S(2)}) %collective-permute-start.5) | collective-permute-done | bytes 327712 | tf_op jit(solution)/shard_map/ppermute | solution.py:188
  42.1 1.7 %hidden_rows.1 = (bf16[192,128]{1,0:T(8,128)(2,1)S(1)}, f32[384,128]{1,0:T(8,128)S(1)}) custom-call(bf16[4,384,1280]{2,1,0:T(8,128)(2,1)S(1)} %weights_in_order.1.panel, bf16[128,1280]{1,0:T(8,128)(2,1)S(1)} %collective-permute-done.1.right, bf16[128,1280]{1,0:T(8,128)(2,1)S(1)} %collective-permute-done.2.left, bf16[128,1280]{1,0:T(8,128)(2,1)S(1)} %own_rows.1.first.here.x, ...), custom_call_target="tpu_custom_call" | custom-call | flops 503316480 | bytes 3932160 | tf_op jit(solution)/shard_map/hidden_rows/pallas_call | solution.py:231
  43.8 2.8 %collective-permute-start.13 = (bf16[192,128]{1,0:T(8,128)(2,1)S(1)}, bf16[192,128]{1,0:T(8,128)(2,1)S(1)}, u32[]{:S(2)}, u32[]{:S(2)}) collective-permute-start(bf16[192,128]{1,0:T(8,128)(2,1)S(1)} %get-tuple-element.18.refs_0_), channel_id=1, source_target_pairs={{0,3},{1,2},{2,1},{3,0},{4,7},{5,6},{6,5},{7,4},{8,11},{9,10},{10,... | collective-permute-start | bytes 147464 | tf_op jit(solution)/shard_map/ppermute | solution.py:151
  46.5 0.3 collective-permute-start.14
  46.8 1.4 %collective-permute-start.15 = (bf16[192,128]{1,0:T(8,128)(2,1)S(1)}, bf16[192,128]{1,0:T(8,128)(2,1)S(1)}, u32[]{:S(2)}, u32[]{:S(2)}) collective-permute-start(bf16[192,128]{1,0:T(8,128)(2,1)S(1)} %get-tuple-element.18.refs_0_), channel_id=1, source_target_pairs={{0,1},{1,0},{2,3},{3,2},{4,5},{5,4},{6,7},{7,6},{8,9},{9,8},{10,11... | collective-permute-start | bytes 147464 | tf_op jit(solution)/shard_map/ppermute | solution.py:151
  48.2 1.1 %collective-permute-done.9.opposite = bf16[128,1280]{1,0:T(8,128)(2,1)S(1)} collective-permute-done((bf16[128,1280]{1,0:T(8,128)(2,1)S(1)}, bf16[128,1280]{1,0:T(8,128)(2,1)S(1)}, u32[]{:S(2)}, u32[]{:S(2)}) %collective-permute-start.9) | collective-permute-done | bytes 327712 | tf_op jit(solution)/shard_map/ppermute | solution.py:188
  49.3 0.0 collective-permute-done.8.x
  49.3 0.7 %last_chunks.1.refs_0_ = bf16[192,128]{1,0:T(8,128)(2,1)S(1)} custom-call(bf16[4,384,1280]{2,1,0:T(8,128)(2,1)S(1)} %weights_in_order.1.panel, f32[384,128]{1,0:T(8,128)S(1)} %get-tuple-element.16.total, bf16[144,1280]{1,0:T(8,128)(2,1)S(1)} %collective-permute-done.8.x, bf16[128,1280]{1,0:T(8,128)(2,1)S(1)} %collective-permute-done.9.opposite), custom_call_target="tpu_custom_call" | custom-call | flops 251658240 | bytes 1966080 | tf_op jit(solution)/shard_map/last_chunks/pallas_call | solution.py:231
  50.0 2.4 %collective-permute-start.11 = (bf16[192,128]{1,0:T(8,128)(2,1)S(1)}, bf16[192,128]{1,0:T(8,128)(2,1)S(1)}, u32[]{:S(2)}, u32[]{:S(2)}) collective-permute-start(bf16[192,128]{1,0:T(8,128)(2,1)S(1)} %last_chunks.1.refs_0_), channel_id=1, source_target_pairs={{0,3},{1,2},{2,1},{3,0},{4,7},{5,6},{6,5},{7,4},{8,11},{9,10},{10,... | collective-permute-start | bytes 147464 | tf_op jit(solution)/shard_map/ppermute | solution.py:151
  52.4 1.5 %collective-permute-start.12 = (bf16[192,128]{1,0:T(8,128)(2,1)S(1)}, bf16[192,128]{1,0:T(8,128)(2,1)S(1)}, u32[]{:S(2)}, u32[]{:S(2)}) collective-permute-start(bf16[192,128]{1,0:T(8,128)(2,1)S(1)} %last_chunks.1.refs_0_), channel_id=1, source_target_pairs={{0,2},{1,3},{2,0},{3,1},{4,6},{5,7},{6,4},{7,5},{8,10},{9,11},{10,... | collective-permute-start | bytes 147464 | tf_op jit(solution)/shard_map/ppermute | solution.py:151
  54.0 0.0 collective-permute-done.13.refs_1_
  54.0 0.5 collective-permute-start.10
  54.5 0.0 collective-permute-done.14.refs_2_
  54.5 0.0 collective-permute-done.15.refs_3_
  54.5 0.0 copy-done
  54.5 1.3 %project_down.2.refs_3_ = bf16[256,1280]{1,0:T(8,128)(2,1)} custom-call(bf16[192,128]{1,0:T(8,128)(2,1)S(1)} %get-tuple-element.18.refs_0_, bf16[192,128]{1,0:T(8,128)(2,1)S(1)} %collective-permute-done.13.refs_1_, bf16[192,128]{1,0:T(8,128)(2,1)S(1)} %collective-permute-done.14.refs_2_, bf16[192,128]{1,0:T(8,128)(2,1)S(1)} %collective-permute-done.15.refs_3_, ...), custom_call_target="tpu_custom_call" | custom-call | flops 8000000000 | bytes 2293760 | tf_op jit(solution)/shard_map/project_down/pallas_call | solution.py:294
  55.8 0.6 %collective-permute-done.11.refs_1_ = bf16[192,128]{1,0:T(8,128)(2,1)S(1)} collective-permute-done((bf16[192,128]{1,0:T(8,128)(2,1)S(1)}, bf16[192,128]{1,0:T(8,128)(2,1)S(1)}, u32[]{:S(2)}, u32[]{:S(2)}) %collective-permute-start.11) | collective-permute-done | bytes 49184 | tf_op jit(solution)/shard_map/ppermute | solution.py:151
  56.4 1.7 %collective-permute-done.12.refs_2_ = bf16[192,128]{1,0:T(8,128)(2,1)S(1)} collective-permute-done((bf16[192,128]{1,0:T(8,128)(2,1)S(1)}, bf16[192,128]{1,0:T(8,128)(2,1)S(1)}, u32[]{:S(2)}, u32[]{:S(2)}) %collective-permute-start.12) | collective-permute-done | bytes 49184 | tf_op jit(solution)/shard_map/ppermute | solution.py:151
  58.1 0.5 early_down.1.refs_2_
  58.5 0.0 collective-permute-done.10.refs_0_
  58.5 1.0 %project_down.3 = bf16[256,1280]{1,0:T(8,128)(2,1)} custom-call(bf16[192,128]{1,0:T(8,128)(2,1)S(1)} %collective-permute-done.10.refs_0_, bf16[768,1280]{1,0:T(8,128)(2,1)S(1)} %bitcast.10, f32[128,1280]{1,0:T(8,128)S(1)} %early_down.1.refs_2_, bf16[256,1280]{1,0:T(8,128)(2,1)} %project_down.2.refs_3_), custom_call_target="tpu_custom_call", output_to_operand_aliasing={{}: (3, {})} | custom-call | flops 125829120 | bytes 2293760 | tf_op jit(solution)/shard_map/project_down/pallas_call | solution.py:294
  (2 shorter events, 0.0 us)
Async XLA Ops:
  1.0 14.8 %collective-permute-start.1 = (bf16[128,1280]{1,0:T(8,128)(2,1)S(1)}, bf16[128,1280]{1,0:T(8,128)(2,1)S(1)}, u32[]{:S(2)}, u32[]{:S(2)}) collective-permute-start(bf16[128,1280]{1,0:T(8,128)(2,1)S(1)} %own_rows.1.first.here.x), channel_id=1, source_target_pairs={{0,1},{1,2},{2,3},{3,0},{4,5},{5,6},{6,7},{7,4},{8,9},{9,10},{10,1... | collective-permute-start | bytes 983048 | tf_op jit(solution)/shard_map/ppermute | solution.py:164
  4.1 21.8 %collective-permute-start.2 = (bf16[128,1280]{1,0:T(8,128)(2,1)S(1)}, bf16[128,1280]{1,0:T(8,128)(2,1)S(1)}, u32[]{:S(2)}, u32[]{:S(2)}) collective-permute-start(bf16[128,1280]{1,0:T(8,128)(2,1)S(1)} %own_rows.1.first.here.x), channel_id=1, source_target_pairs={{0,3},{1,0},{2,1},{3,2},{4,7},{5,4},{6,5},{7,6},{8,11},{9,8},{10,9... | collective-permute-start | bytes 983048 | tf_op jit(solution)/shard_map/ppermute | solution.py:165
  7.5 23.3 %collective-permute-start = (bf16[384,1280]{1,0:T(8,128)(2,1)S(1)}, bf16[384,1280]{1,0:T(8,128)(2,1)S(1)}, u32[]{:S(2)}, u32[]{:S(2)}) collective-permute-start(bf16[384,1280]{1,0:T(8,128)(2,1)S(1)} %get-tuple-element.14.refs_0_), channel_id=1, source_target_pairs={{0,16},{8,24},{16,0},{24,8},{1,17},{9,25},{17,1},{25,9},{2,18},{10... | collective-permute-start | bytes 2949128 | tf_op jit(solution)/shard_map/ppermute | solution.py:151
  9.2 21.5 %collective-permute-start.6 = (bf16[128,1280]{1,0:T(8,128)(2,1)S(1)}, bf16[128,1280]{1,0:T(8,128)(2,1)S(1)}, u32[]{:S(2)}, u32[]{:S(2)}) collective-permute-start(bf16[128,1280]{1,0:T(8,128)(2,1)S(1)} %get-tuple-element.15.here), channel_id=1, source_target_pairs={{0,5},{1,6},{2,7},{3,4},{4,1},{5,2},{6,3},{7,0},{8,13},{9,14},{10,... | collective-permute-start | bytes 983048 | tf_op jit(solution)/shard_map/ppermute | solution.py:164
  9.9 26.1 %collective-permute-start.7 = (bf16[128,1280]{1,0:T(8,128)(2,1)S(1)}, bf16[128,1280]{1,0:T(8,128)(2,1)S(1)}, u32[]{:S(2)}, u32[]{:S(2)}) collective-permute-start(bf16[128,1280]{1,0:T(8,128)(2,1)S(1)} %get-tuple-element.15.here), channel_id=1, source_target_pairs={{0,7},{1,4},{2,5},{3,6},{4,3},{5,0},{6,1},{7,2},{8,15},{9,12},{10,... | collective-permute-start | bytes 983048 | tf_op jit(solution)/shard_map/ppermute | solution.py:165
  13.9 0.7 %copy-start.1 = (bf16[256]{0:T(256)(128)(2,1)S(1)}, bf16[256]{0:T(256)(128)(2,1)}, u32[]{:S(2)}) copy-start(bf16[256]{0:T(256)(128)(2,1)} %param.7) | copy-start | bytes 1540
  14.6 0.7 %copy-start.2 = (s32[2]{0:T(128)S(1)}, s32[2]{0:T(128)}, u32[]{:S(2)}) copy-start(s32[2]{0:T(128)} %counts.1) | copy-start | bytes 28
  26.0 16.1 %collective-permute-start.5 = (bf16[128,1280]{1,0:T(8,128)(2,1)S(1)}, bf16[128,1280]{1,0:T(8,128)(2,1)S(1)}, u32[]{:S(2)}, u32[]{:S(2)}) collective-permute-start(bf16[128,1280]{1,0:T(8,128)(2,1)S(1)} %choose.2), channel_id=1, source_target_pairs={{0,2},{3,1},{2,3},{1,0},{4,6},{7,5},{6,7},{5,4},{8,10},{11,9},{10,... | collective-permute-start | bytes 983048 | tf_op jit(solution)/shard_map/ppermute | solution.py:188
  27.0 22.3 %collective-permute-start.8 = (bf16[144,1280]{1,0:T(8,128)(2,1)S(1)}, bf16[144,1280]{1,0:T(8,128)(2,1)S(1)}, u32[]{:S(2)}, u32[]{:S(2)}) collective-permute-start(bf16[144,1280]{1,0:T(8,128)(2,1)S(1)} %attach_weights.1), channel_id=1, source_target_pairs={{0,4},{4,0},{1,5},{5,1},{2,6},{6,2},{3,7},{7,3},{8,12},{12,8},{9,1... | collective-permute-start | bytes 1105928 | tf_op jit(solution)/shard_map/ppermute | solution.py:323
  30.7 6.9 %collective-permute-start.4 = (bf16[384,1280]{1,0:T(8,128)(2,1)S(1)}, bf16[384,1280]{1,0:T(8,128)(2,1)S(1)}, u32[]{:S(2)}, u32[]{:S(2)}) collective-permute-start(bf16[384,1280]{1,0:T(8,128)(2,1)S(1)} %collective-permute-done.refs_2_), channel_id=1, source_target_pairs={{0,8},{8,0},{16,24},{24,16},{1,9},{9,1},{17,25},{25,17},{2,10},{10... | collective-permute-start | bytes 2949128 | tf_op jit(solution)/shard_map/ppermute | solution.py:151
  30.8 6.9 %collective-permute-start.3 = (bf16[384,1280]{1,0:T(8,128)(2,1)S(1)}, bf16[384,1280]{1,0:T(8,128)(2,1)S(1)}, u32[]{:S(2)}, u32[]{:S(2)}) collective-permute-start(bf16[384,1280]{1,0:T(8,128)(2,1)S(1)} %get-tuple-element.14.refs_0_), channel_id=1, source_target_pairs={{0,8},{8,0},{16,24},{24,16},{1,9},{9,1},{17,25},{25,17},{2,10},{10... | collective-permute-start | bytes 2949128 | tf_op jit(solution)/shard_map/ppermute | solution.py:151
  36.1 13.2 %collective-permute-start.9 = (bf16[128,1280]{1,0:T(8,128)(2,1)S(1)}, bf16[128,1280]{1,0:T(8,128)(2,1)S(1)}, u32[]{:S(2)}, u32[]{:S(2)}) collective-permute-start(bf16[128,1280]{1,0:T(8,128)(2,1)S(1)} %choose.3), channel_id=1, source_target_pairs={{0,6},{3,5},{2,3},{1,0},{4,2},{7,1},{6,7},{5,4},{8,14},{11,13},{10... | collective-permute-start | bytes 983048 | tf_op jit(solution)/shard_map/ppermute | solution.py:188
  38.9 15.6 %copy-start = (bf16[1,768,1280]{2,1,0:T(8,128)(2,1)S(1)}, bf16[1,768,1280]{2,1,0:T(8,128)(2,1)}, u32[]{:S(2)}) copy-start(bf16[1,768,1280]{2,1,0:T(8,128)(2,1)} %param.11) | copy-start | bytes 5898244
  43.8 10.2 %collective-permute-start.13 = (bf16[192,128]{1,0:T(8,128)(2,1)S(1)}, bf16[192,128]{1,0:T(8,128)(2,1)S(1)}, u32[]{:S(2)}, u32[]{:S(2)}) collective-permute-start(bf16[192,128]{1,0:T(8,128)(2,1)S(1)} %get-tuple-element.18.refs_0_), channel_id=1, source_target_pairs={{0,3},{1,2},{2,1},{3,0},{4,7},{5,6},{6,5},{7,4},{8,11},{9,10},{10,... | collective-permute-start | bytes 147464 | tf_op jit(solution)/shard_map/ppermute | solution.py:151
  46.5 7.9 %collective-permute-start.14 = (bf16[192,128]{1,0:T(8,128)(2,1)S(1)}, bf16[192,128]{1,0:T(8,128)(2,1)S(1)}, u32[]{:S(2)}, u32[]{:S(2)}) collective-permute-start(bf16[192,128]{1,0:T(8,128)(2,1)S(1)} %get-tuple-element.18.refs_0_), channel_id=1, source_target_pairs={{0,2},{1,3},{2,0},{3,1},{4,6},{5,7},{6,4},{7,5},{8,10},{9,11},{10,... | collective-permute-start | bytes 147464 | tf_op jit(solution)/shard_map/ppermute | solution.py:151
  46.8 7.7 %collective-permute-start.15 = (bf16[192,128]{1,0:T(8,128)(2,1)S(1)}, bf16[192,128]{1,0:T(8,128)(2,1)S(1)}, u32[]{:S(2)}, u32[]{:S(2)}) collective-permute-start(bf16[192,128]{1,0:T(8,128)(2,1)S(1)} %get-tuple-element.18.refs_0_), channel_id=1, source_target_pairs={{0,1},{1,0},{2,3},{3,2},{4,5},{5,4},{6,7},{7,6},{8,9},{9,8},{10,11... | collective-permute-start | bytes 147464 | tf_op jit(solution)/shard_map/ppermute | solution.py:151
  50.0 6.4 %collective-permute-start.11 = (bf16[192,128]{1,0:T(8,128)(2,1)S(1)}, bf16[192,128]{1,0:T(8,128)(2,1)S(1)}, u32[]{:S(2)}, u32[]{:S(2)}) collective-permute-start(bf16[192,128]{1,0:T(8,128)(2,1)S(1)} %last_chunks.1.refs_0_), channel_id=1, source_target_pairs={{0,3},{1,2},{2,1},{3,0},{4,7},{5,6},{6,5},{7,4},{8,11},{9,10},{10,... | collective-permute-start | bytes 147464 | tf_op jit(solution)/shard_map/ppermute | solution.py:151
  52.4 5.6 %collective-permute-start.12 = (bf16[192,128]{1,0:T(8,128)(2,1)S(1)}, bf16[192,128]{1,0:T(8,128)(2,1)S(1)}, u32[]{:S(2)}, u32[]{:S(2)}) collective-permute-start(bf16[192,128]{1,0:T(8,128)(2,1)S(1)} %last_chunks.1.refs_0_), channel_id=1, source_target_pairs={{0,2},{1,3},{2,0},{3,1},{4,6},{5,7},{6,4},{7,5},{8,10},{9,11},{10,... | collective-permute-start | bytes 147464 | tf_op jit(solution)/shard_map/ppermute | solution.py:151
  54.0 4.6 %collective-permute-start.10 = (bf16[192,128]{1,0:T(8,128)(2,1)S(1)}, bf16[192,128]{1,0:T(8,128)(2,1)S(1)}, u32[]{:S(2)}, u32[]{:S(2)}) collective-permute-start(bf16[192,128]{1,0:T(8,128)(2,1)S(1)} %last_chunks.1.refs_0_), channel_id=1, source_target_pairs={{0,1},{1,0},{2,3},{3,2},{4,5},{5,4},{6,7},{7,6},{8,9},{9,8},{10,11... | collective-permute-start | bytes 147464 | tf_op jit(solution)/shard_map/ppermute | solution.py:151
